TPU v7x, 256 devices: a whole 4x4x8 slice. The times are simulated.
256 devices in a mesh: row: 32 (over x, y, core), col: 8 (over z).
Axes of the slice: x: 4, y: 4, z: 8, core: 2. Of those that a mesh axis runs over, the one named last changes fastest.
Arguments:
- rhs: float32 [64, 16384], P(None, 'row'), may hold values from -60 to 60
- near_flags: int32 [32, 32], P('row', 'col'), may hold values from 0 to 1, as said below
- near_blocks: bfloat16 [32, 32, 512, 512], P('row', 'col'), may hold values from -0.0625 to 0.0625
- far_columns: bfloat16 [32, 32, 64, 512], P('row', 'col'), may hold values from -0.25 to 0.25
- row_basis: bfloat16 [32, 64, 512], P('row'), may hold values from -0.125 to 0.125
- self_term: float32 [16384], P('row'), may hold values from 1.5 to 3
- diag_inverse: float32 [32, 512, 512], P('row'), may hold values from -2 to 2
- lower_block: float32 [32, 512, 512], P('row'), may hold values from -3 to 3
Outputs:
- solution: float32 [64, 16384], P(None, 'row')
Inputs may be any that keep to these rules, and one draw needn't show every extreme that they name: near_flags[i, i] and near_flags[i, i - 1], near_flags[i, i + 1] are 1.
All inputs are finite; a program needn't handle non-finite values.
Results may differ from a plain program's by a relative error of at most 0.00065.
Values may be sent and summed in bfloat16 or wider, within the bound.
A program may use at most 128 MiB of HBM per device.

v0:
```python
import jax
import jax.numpy as jnp
from jax import lax
from jax.sharding import PartitionSpec as P

epsilon = 1e-06
highest = lax.Precision.HIGHEST


def from_behind(block, axis, distance):
    devices = range(lax.axis_size(axis))
    route = [(i - distance, i) for i in devices if i - distance in devices]
    return lax.ppermute(block, axis, route)


def column_total(left_vec, right_vec):
    return jnp.sum(left_vec * right_vec, axis=1)


def column_norm(vector):
    return jnp.sqrt(lax.psum(column_total(vector, vector), "row") + epsilon)


def apply_matrix(solved, near_flags, near_blocks, far_columns, row_basis, self_term):
    gathered = lax.all_gather(solved.astype(jnp.bfloat16), "row", axis=1, tiled=True)
    local_count = near_blocks.shape[1]
    cluster = near_blocks.shape[2]
    systems = solved.shape[0]
    offset = lax.axis_index("col") * (local_count * cluster)
    own_inputs = lax.dynamic_slice_in_dim(gathered, offset, local_count * cluster, 1)
    own_inputs = own_inputs.reshape(systems, local_count, cluster)
    weight = near_flags[0].astype(jnp.bfloat16)
    near_in = own_inputs * weight[None, :, None]
    far_in = own_inputs - near_in
    near_part = jnp.einsum(
        "skb,kbd->sd", near_in, near_blocks[0], preferred_element_type=jnp.float32
    )
    far_coef = jnp.einsum("skb,krb->sr", far_in, far_columns[0], preferred_element_type=jnp.float32)
    near_part, far_coef = lax.psum((near_part, far_coef), "col")
    far_part = jnp.dot(
        far_coef.astype(jnp.bfloat16), row_basis[0], preferred_element_type=jnp.float32
    )
    return self_term[None, :] * solved + near_part + far_part


def precondition(vector, inverse, lower):
    start = jnp.dot(vector, inverse, precision=highest)

    def advance(iteration, current):
        previous = from_behind(current, "row", 1)
        return jnp.dot(
            vector - jnp.dot(previous, lower, precision=highest), inverse, precision=highest
        )

    return lax.fori_loop(0, lax.axis_size("row") - 1, advance, start)


def project(basis_list, image):
    heights = []
    for direction in basis_list:
        height = lax.psum(column_total(direction, image), "row")
        image = image - height[:, None] * direction
        heights.append(height)
    return (heights, image)


def least_squares(beta, proj_one, norm_one, cross, proj_two, norm_two):
    radius_one = jnp.sqrt(proj_one * proj_one + norm_one * norm_one)
    cos_one = proj_one / radius_one
    sin_one = norm_one / radius_one
    upper = cos_one * cross + sin_one * proj_two
    middle = cos_one * proj_two - sin_one * cross
    radius_two = jnp.sqrt(middle * middle + norm_two * norm_two)
    weight_two = -(middle / radius_two) * sin_one * beta / radius_two
    weight_one = (cos_one * beta - upper * weight_two) / radius_one
    return (weight_one, weight_two)


def body(
    rhs, near_flags, near_blocks, far_columns, row_basis, self_term, diag_inverse, lower_block
):
    inverse = diag_inverse[0]
    lower = lower_block[0]
    beta = column_norm(rhs)
    first = rhs / beta[:, None]
    pre_one = precondition(first, inverse, lower)
    image = apply_matrix(pre_one, near_flags, near_blocks, far_columns, row_basis, self_term)
    heights, image = project([first], image)
    proj_one = heights[0]
    norm_one = column_norm(image)
    second = image / norm_one[:, None]
    pre_two = precondition(second, inverse, lower)
    image = apply_matrix(pre_two, near_flags, near_blocks, far_columns, row_basis, self_term)
    heights, image = project([first, second], image)
    cross = heights[0]
    proj_two = heights[1]
    norm_two = column_norm(image)
    weight_one, weight_two = least_squares(beta, proj_one, norm_one, cross, proj_two, norm_two)
    return pre_one * weight_one[:, None] + pre_two * weight_two[:, None]


def solution(mesh):
    placed = (
        P(None, "row"),
        P("row", "col"),
        P("row", "col", None, None),
        P("row", "col", None, None),
        P("row", None, None),
        P("row"),
        P("row", None, None),
        P("row", None, None),
    )
    return jax.shard_map(
        body, mesh=mesh, in_specs=placed, out_specs=P(None, "row"), check_vma=False
    )
```

profile of v0, /device:TPU:1, one launch (start us, length us, event | category | flops | bytes accessed | tf_op | source)
XLA Modules:
  0.0 1353.2 jit_solution(18100743485379574816)
XLA Ops:
  7.7 65.3 %psum.70 = f32[64]{0:T(128)S(1)} all-reduce(f32[64]{0:T(128)S(1)} %multiply_reduce_fusion.5), channel_id=1, replica_groups=mesh['row'=32,'col'=8] {'row'}, use_global_device_ids=true, to_apply=%region_1.0 | all-reduce | flops 64 | bytes 512 | tf_op jit(solution)/shard_map/psum | solution.py:21
  77.0 312.3 %while.20 = (s32[]{:T(128)}, f32[64,512]{1,0:T(8,128)S(1)}, f32[512,512]{1,0:T(8,128)}, f32[64,512]{1,0:T(8,128)S(1)}, f32[512,512]{1,0:T(8,128)}, /*index=5*/s32[]{:T(128)}) while((s32[]{:T(128)}, f32[64,512]{1,0:T(8,128)S(1)}, f32[512,512]{1,0:T(8,128)}, f32[64,512]{1,0:T(8,128)S(1)}, f32[512,512]{1,0:T(8,128)}, /*index=5*/s32[]{:T(128)}) %tuple.52), condition=%wide.region_3.0_spmd, body=%wide.region_2.0_spmd.sunk | while | flops 402685952 | bytes 7471241 | solution.py:55
  231.3 6.6 collective-permute-start
  242.6 6.6 collective-permute-start
  253.9 6.6 collective-permute-start
  265.2 6.6 collective-permute-start
  276.5 6.6 collective-permute-start
  287.8 6.6 collective-permute-start
  299.1 6.6 collective-permute-start
  310.3 6.6 collective-permute-start
  321.6 6.6 collective-permute-start
  332.9 6.6 collective-permute-start
  344.2 6.6 collective-permute-start
  355.5 6.6 collective-permute-start
  366.8 6.6 collective-permute-start
  378.1 6.6 collective-permute-start
  390.1 79.2 %all-gather.3.cloned.1.call-done = bf16[64,16384]{1,0:T(8,128)(2,1)} async-done(((bf16[64,512]{1,0:T(8,128)(2,1)}), bf16[64,16384]{1,0:T(8,128)(2,1)}) %all-gather.3.cloned.1.call-update) | async-done | bytes 2097168 | tf_op jit(solution)/shard_map/all_gather | solution.py:25
  474.4 24.4 %psum.72 = bf16[64,64]{1,0:T(8,128)(2,1)S(1)} all-reduce(f32[64,64]{1,0:T(8,128)} %convolution_bitcast_fusion.1), channel_id=1, replica_groups=mesh['row'=32,'col'=8] {'col'}, use_global_device_ids=true, to_apply=%region_5.0 | all-reduce | flops 4096 | bytes 24576 | tf_op jit(solution)/shard_map/psum | solution.py:39
  498.8 39.9 %all-reduce.3.cloned.1.call-done = f32[64,512]{1,0:T(8,128)} async-done(((f32[64,512]{1,0:T(8,128)}), f32[64,512]{1,0:T(8,128)}) %all-reduce.3.cloned.1.call-update) | async-done | bytes 131088 | tf_op jit(solution)/shard_map/psum | solution.py:39
  541.0 67.7 %psum.73 = f32[64]{0:T(128)S(1)} all-reduce(f32[64]{0:T(128)} %get-tuple-element.87), channel_id=1, replica_groups=mesh['row'=32,'col'=8] {'row'}, use_global_device_ids=true, to_apply=%region_7.0 | all-reduce | flops 64 | bytes 512 | tf_op jit(solution)/shard_map/psum | solution.py:61
  609.8 62.7 %psum.74 = f32[64]{0:T(128)S(1)} all-reduce(f32[64]{0:T(128)S(1)} %multiply_reduce_fusion.3), channel_id=1, replica_groups=mesh['row'=32,'col'=8] {'row'}, use_global_device_ids=true, to_apply=%region_9.0 | all-reduce | flops 64 | bytes 512 | tf_op jit(solution)/shard_map/psum | solution.py:21
  675.0 332.6 %while.21 = (s32[]{:T(128)}, f32[64,512]{1,0:T(8,128)}, f32[512,512]{1,0:T(8,128)}, f32[64,512]{1,0:T(8,128)S(1)}, f32[512,512]{1,0:T(8,128)S(1)}, /*index=5*/s32[]{:T(128)}) while((s32[]{:T(128)}, f32[64,512]{1,0:T(8,128)}, f32[512,512]{1,0:T(8,128)}, f32[64,512]{1,0:T(8,128)S(1)}, f32[512,512]{1,0:T(8,128)S(1)}, /*index=5*/s32[]{:T(128)}) %tuple.53), condition=%wide.region_11.0_spmd, body=%wide.region_10.0_spmd.sunk | while | flops 402685952 | bytes 3276909 | solution.py:55
  885.8 6.5 collective-permute-start.1
  898.0 6.5 collective-permute-start.1
  971.0 6.5 collective-permute-start.1
  983.2 6.5 collective-permute-start.1
  1009.2 73.3 %all-gather.5.cloned.1.call-done = bf16[64,16384]{1,0:T(8,128)(2,1)} async-done(((bf16[64,512]{1,0:T(8,128)(2,1)}), bf16[64,16384]{1,0:T(8,128)(2,1)}) %all-gather.5.cloned.1.call-update) | async-done | bytes 2097168 | tf_op jit(solution)/shard_map/all_gather | solution.py:25
  1085.3 23.9 %psum.76 = bf16[64,64]{1,0:T(8,128)(2,1)S(1)} all-reduce(f32[64,64]{1,0:T(8,128)S(1)} %convolution_bitcast_fusion), channel_id=1, replica_groups=mesh['row'=32,'col'=8] {'col'}, use_global_device_ids=true, to_apply=%region_13.0 | all-reduce | flops 4096 | bytes 24576 | tf_op jit(solution)/shard_map/psum | solution.py:39
  1109.2 42.0 %all-reduce.5.cloned.1.call-done = f32[64,512]{1,0:T(8,128)} async-done(((f32[64,512]{1,0:T(8,128)}), f32[64,512]{1,0:T(8,128)}) %all-reduce.5.cloned.1.call-update) | async-done | bytes 131088 | tf_op jit(solution)/shard_map/psum | solution.py:39
  1152.4 67.7 %psum.77 = f32[64]{0:T(128)S(1)} all-reduce(f32[64]{0:T(128)S(1)} %get-tuple-element.89), channel_id=1, replica_groups=mesh['row'=32,'col'=8] {'row'}, use_global_device_ids=true, to_apply=%region_15.0 | all-reduce | flops 64 | bytes 512 | tf_op jit(solution)/shard_map/psum | solution.py:61
  1220.3 62.7 %psum.78 = f32[64]{0:T(128)S(1)} all-reduce(f32[64]{0:T(128)S(1)} %multiply_reduce_fusion.1), channel_id=1, replica_groups=mesh['row'=32,'col'=8] {'row'}, use_global_device_ids=true, to_apply=%region_17.0 | all-reduce | flops 64 | bytes 512 | tf_op jit(solution)/shard_map/psum | solution.py:61
  1283.1 62.7 %psum.79 = f32[64]{0:T(128)S(1)} all-reduce(f32[64]{0:T(128)S(1)} %multiply_reduce_fusion), channel_id=1, replica_groups=mesh['row'=32,'col'=8] {'row'}, use_global_device_ids=true, to_apply=%region_19.0 | all-reduce | flops 64 | bytes 512 | tf_op jit(solution)/shard_map/psum | solution.py:21
  (361 shorter events, 548.8 us)
Async XLA Ops:
  6.5 462.8 %all-gather.3.cloned.1.call-start = ((), (), s32[]{:S(2)}) async-start(), calls=%async_computation | async-start | bytes 2162688 | tf_op jit(solution)/shard_map/all_gather | solution.py:25
  221.5 7.1 collective-permute-start
  231.3 8.5 collective-permute-start
  242.6 8.5 collective-permute-start
  253.9 8.5 collective-permute-start
  265.2 8.5 collective-permute-start
  276.5 8.5 collective-permute-start
  287.8 8.5 collective-permute-start
  299.1 8.5 collective-permute-start
  310.3 8.5 collective-permute-start
  321.6 8.5 collective-permute-start
  332.9 8.5 collective-permute-start
  344.2 8.5 collective-permute-start
  355.5 8.5 collective-permute-start
  366.8 8.5 collective-permute-start
  378.1 8.5 collective-permute-start
  390.0 148.6 %all-reduce.3.cloned.1.call-start = ((), (), s32[]{:S(2)}) async-start(), calls=%async_computation.1 | async-start | bytes 262144 | tf_op jit(solution)/shard_map/psum | solution.py:39
  472.5 609.9 %all-gather.5.cloned.1.call-start = ((), (), s32[]{:S(2)}) async-start(), calls=%async_computation.2 | async-start | bytes 2162688 | tf_op jit(solution)/shard_map/all_gather | solution.py:25
  692.8 6.6 collective-permute-start.1
  712.9 6.6 collective-permute-start.1
  874.0 8.3 collective-permute-start.1
  885.8 8.7 collective-permute-start.1
  898.0 8.7 collective-permute-start.1
  910.2 8.7 collective-permute-start.1
  922.3 8.7 collective-permute-start.1
  934.5 8.7 collective-permute-start.1
  946.7 8.7 collective-permute-start.1
  958.9 8.7 collective-permute-start.1
  971.0 8.7 collective-permute-start.1
  983.2 8.7 collective-permute-start.1
  995.4 8.7 collective-permute-start.1
  1009.1 142.1 %all-reduce.5.cloned.1.call-start = ((), (), s32[]{:S(2)}) async-start(), calls=%async_computation.3 | async-start | bytes 262144 | tf_op jit(solution)/shard_map/psum | solution.py:39
  (82 other events, 3125.6 us)
Sparse Core Ops, SparseCore 0:
  390.2 79.0 all-gather.2
  472.7 65.9 all-reduce.2
  1009.2 73.1 all-gather.4
  1085.2 65.9 all-reduce.4
where the time goes:
time: 1360 us; the launch traced here: 1350 us
  blocking collectives  437 us (32%)
  waiting for transfers between devices  365 us (27%)
  starting transfers between devices  320 us (24%)
  matrix products  203 us (15%)
    ppermute x62, starting transfers between devices, from_behind(): return lax.ppermute(block, axis, route)  320 us
    psum x3, blocking collectives, project(): height = lax.psum(column_total(direction, image), 'row')  198 us
    psum x3, blocking collectives, column_norm(): return jnp.sqrt(lax.psum(column_total(vector, vector), 'row') + epsilon)  191 us
    all_gather x2, waiting for transfers between devices, apply_matrix(): lax.all_gather(solved.astype(jnp.bfloat16), 'row', axis=1, tiled=True)  152 us
    ppermute x62, waiting for transfers between devices, from_behind(): return lax.ppermute(block, axis, route)  131 us
    dot_general x62, matrix products, advance(): jnp.dot(previous, lower, precision=highest)  125 us
    psum x2, waiting for transfers between devices, apply_matrix(): near_part, far_coef = lax.psum((near_part, far_coef), 'col')  81.9 us
    dot_general x62, matrix products, advance(): jnp.dot(vector - jnp.dot(previous, lower, precision=highest), inverse, pr...  67.4 us
  transfers between devices with their start and end apart: 66, of which 66 were waited for; matrix products, arithmetic and copies ran while one was open for 0% of the time, Pallas kernels for 0%

commit v1 on v0

v1 whole, which is shorter than its diff:
```python
import functools

import jax
import jax.numpy as jnp
from jax import lax
from jax.experimental import pallas as pl
from jax.experimental.pallas import tpu as pltpu
from jax.sharding import PartitionSpec as P

epsilon = 1e-06
f32 = jnp.float32
bf16 = jnp.bfloat16
MESH = pl.DeviceIdType.MESH
SYS = 8


def stacked(x):
    high = x.astype(bf16).astype(f32)
    return jnp.concatenate([high, x - high], axis=0).astype(bf16)


def times(x, mat):
    y = jnp.dot(stacked(x), mat, preferred_element_type=f32)
    n, c = x.shape[0], mat.shape[1] // 2
    y = y[:n] + y[n:]
    return y[:, :c] + y[:, c:]


def put_split(ref, rows, m):
    c = m.shape[1]
    high = m.astype(bf16)
    ref[rows, :c] = high
    ref[rows, c:] = (m - high.astype(f32)).astype(bf16)


def total(x):
    return jnp.sum(x, axis=1, keepdims=True)


def least_squares(beta, proj_one, norm_one, cross, proj_two, norm_two):
    radius_one = jnp.sqrt(proj_one * proj_one + norm_one * norm_one)
    cos_one = proj_one / radius_one
    sin_one = norm_one / radius_one
    upper = cos_one * cross + sin_one * proj_two
    middle = cos_one * proj_two - sin_one * cross
    radius_two = jnp.sqrt(middle * middle + norm_two * norm_two)
    weight_two = -(middle / radius_two) * sin_one * beta / radius_two
    weight_one = (cos_one * beta - upper * weight_two) / radius_one
    return (weight_one, weight_two)


def kernel(
    rows, cols, tile,
    rhs, flags, near, far, basis, selft, dinv, low, out,
    dsp, mats, m0, crecv, csend, ebuf, prev, pcur, piece, zbuf, pbuf, part, stile, gath, fsend, fin,
    m_send, m_recv, c_send, c_recv, p_send, p_recv, z_send, z_recv, r_send, r_recv, g_send, g_recv,
    f_send, f_recv,
):
    row = lax.axis_index("row")
    col = lax.axis_index("col")
    chip = row // 2
    core = row % 2
    last = rows // 2 - 1
    per = rows // cols
    home = row // per
    c = dinv.shape[-1]
    half = c // 2
    rank = basis.shape[1]

    bar = pltpu.get_barrier_semaphore()

    def tell(r, k):
        pl.semaphore_signal(bar, inc=1, device_id=(r, k), device_id_type=MESH)

    @pl.loop(1, rows)
    def _(t):
        tell(lax.rem(row + t, rows), col)

    @pl.loop(1, cols)
    def _(t):
        tell(row, lax.rem(col + t, cols))

    @pl.loop(0, rows)
    def _(t):
        r = per * col + t // cols
        k = t % cols

        @pl.when(jnp.logical_or(r != row, k != col))
        def _():
            tell(r, k)

    @pl.when(chip > 0)
    def _():
        tell(2 * chip - 1, col)

    @pl.when(core == 1)
    def _():
        tell(row - 1, col)

    expected = (rows - 1) + (cols - 1) + rows
    expected = expected - jnp.where(home == col, 1, 0)
    expected = expected + jnp.where(core == 0, 1, jnp.where(chip < last, 2, 0))
    pl.semaphore_wait(bar, expected)

    def spread(turn):
        @pl.loop(1, rows)
        def _(t):
            pltpu.make_async_remote_copy(
                src_ref=stile.at[turn], dst_ref=gath.at[turn, t - 1],
                send_sem=g_send.at[turn], recv_sem=g_recv.at[turn],
                device_id=(lax.rem(row + t, rows), col), device_id_type=MESH,
            ).start()

    def arrive(turn):
        pltpu.make_async_copy(gath.at[turn], gath.at[turn], g_recv.at[turn]).wait()

    v = rhs[pl.ds(pl.multiple_of(col * SYS, SYS), SYS), :]
    stile[0] = jnp.broadcast_to(total(v * v), (SYS, 128))
    spread(0)

    @pl.loop(0, c // tile)
    def _(t):
        at = pl.ds(pl.multiple_of(t * tile, tile), tile)
        put_split(dsp, at, dinv[0, at, :])

    place = 1 - core

    def to_sibling(t):
        at = pl.ds(pl.multiple_of(t * tile, tile), tile)
        return pltpu.make_async_remote_copy(
            src_ref=mats.at[1, at], dst_ref=m0.at[at],
            send_sem=m_send.at[t], recv_sem=m_recv.at[t],
            device_id=(row - core + 1, col), device_id_type=MESH,
        )

    @pl.loop(0, c // tile)
    def _(t):
        at = pl.ds(pl.multiple_of(t * tile, tile), tile)
        put_split(mats.at[place], at, times(low[0, at, :], dsp[...]))

        @pl.when(core == 0)
        def _():
            to_sibling(t).start()

    @pl.when(core == 1)
    def _():
        @pl.loop(0, c // tile)
        def _(t):
            to_sibling(t).wait_recv()
            at = pl.ds(pl.multiple_of(t * tile, tile), tile)
            both = jnp.concatenate([m0[at, :c], m0[at, c:]], axis=0)
            y = jnp.dot(both, mats[0], preferred_element_type=f32)
            y = y[:tile] + y[tile:]
            put_split(mats.at[1], at, y[:, :c] + y[:, c:])

    sign = jnp.where(core == 0, -1.0, 1.0).astype(f32)

    def c_copy(app):
        return pltpu.make_async_remote_copy(
            src_ref=csend.at[app], dst_ref=crecv.at[app],
            send_sem=c_send.at[app], recv_sem=c_recv.at[app],
            device_id=(row - core + 1, col), device_id_type=MESH,
        )

    def p_copy(app, to):
        return pltpu.make_async_remote_copy(
            src_ref=pcur.at[app], dst_ref=prev.at[app],
            send_sem=p_send.at[app, to], recv_sem=p_recv.at[app],
            device_id=(2 * chip + 2 + to, col), device_id_type=MESH,
        )

    def chain(app, vec):
        own = times(vec, dsp[...])

        @pl.when(core == 0)
        def _():
            csend[app] = own
            c_copy(app).start()
            ebuf[...] = own

        @pl.when(core == 1)
        def _():
            c_copy(app).wait_recv()
            ebuf[...] = own - times(crecv[app], mats[0])

        @pl.when(chip == 0)
        def _():
            pcur[app] = ebuf[...]

        @pl.when(chip > 0)
        def _():
            p_copy(app, 0).wait_recv()
            pcur[app] = ebuf[...] + sign * times(prev[app], mats[1])

        @pl.when(jnp.logical_and(core == 1, chip < last))
        def _():
            p_copy(app, 1).start()
            p_copy(app, 0).start()

    def z_copy(app, t):
        return pltpu.make_async_remote_copy(
            src_ref=piece.at[app], dst_ref=zbuf.at[app, lax.rem(row, per), col],
            send_sem=z_send.at[app, t], recv_sem=z_recv.at[app, lax.rem(row, per)],
            device_id=(lax.rem(row + t, rows), home), device_id_type=MESH,
        )

    def r_copy(app, t):
        to = lax.rem(col + t, cols)
        return pltpu.make_async_remote_copy(
            src_ref=pbuf.at[app, to], dst_ref=part.at[app, t - 1],
            send_sem=r_send.at[app], recv_sem=r_recv.at[app],
            device_id=(row, to), device_id_type=MESH,
        )

    def apply_matrix(app, pre):
        piece[app] = jnp.concatenate([pre[:, :half], pre[:, half:]], axis=0).astype(bf16)

        @pl.when(home == col)
        def _():
            pltpu.make_async_copy(
                piece.at[app], zbuf.at[app, lax.rem(row, per), col], z_recv.at[app, lax.rem(row, per)]
            ).start()

        @pl.when(home != col)
        def _():
            z_copy(app, 0).start()

        @pl.loop(1, rows)
        def _(t):
            z_copy(app, t).start()

        near_sum = jnp.zeros((SYS * cols, c), f32)
        far_sum = jnp.zeros((SYS * cols, rank), f32)
        for j in range(per):
            pltpu.make_async_copy(zbuf.at[app, j], zbuf.at[app, j], z_recv.at[app, j]).wait()
            z = zbuf[app, j].astype(f32)
            z = jnp.concatenate(
                [z[:, :SYS].reshape(SYS * cols, half), z[:, SYS:].reshape(SYS * cols, half)], axis=1
            )
            near_in = z * flags[0, j].astype(f32)
            far_in = (z - near_in).astype(bf16)
            near_sum += jnp.dot(near_in.astype(bf16), near[0, j], preferred_element_type=f32)
            far_sum += lax.dot_general(
                far_in, far[0, j], (((1,), (1,)), ((), ())), preferred_element_type=f32
            )
        pbuf[app, :, :, :c] = near_sum.reshape(cols, SYS, c)
        pbuf[app, :, :, c:] = jnp.concatenate(
            [far_sum, jnp.zeros((SYS * cols, 128 - rank), f32)], axis=1
        ).reshape(cols, SYS, 128)

        @pl.loop(1, cols)
        def _(t):
            r_copy(app, t).start()

        pltpu.make_async_copy(part.at[app], part.at[app], r_recv.at[app]).wait()
        both = pbuf[app, col]
        for t in range(cols - 1):
            both += part[app, t]
        far_part = jnp.dot(
            both[:, c:c + rank].astype(bf16), basis[0], preferred_element_type=f32
        )
        return selft[...] * pre + both[:, :c] + far_part

    lane = lax.broadcasted_iota(jnp.int32, (SYS, 128), 1)

    arrive(0)
    own_square = stile[0]
    squares = own_square
    for t in range(rows - 1):
        squares += gath[0, t]
    beta_tile = jnp.sqrt(squares + epsilon)
    beta = beta_tile[:, :1]
    first = v / beta
    chain(0, first)
    pre_one = pcur[0]
    image = apply_matrix(0, pre_one)

    def along(size):
        return jnp.sqrt(size) / beta_tile

    root = along(own_square)[:, :1]
    height = total(first * image)
    some = root > 1e-15
    scaled = jnp.where(some, height / jnp.where(some, root, 1.0), 0.0)
    slope = jnp.where(some, scaled / jnp.where(some, root, 1.0), 0.0)
    left = image - slope * first
    rest = jnp.sqrt(total(left * left))
    stile[1] = jnp.where(lane == 0, height, jnp.where(lane == 1, scaled, jnp.where(lane == 2, rest, 0.0)))

    @pl.when(chip > 0)
    def _():
        spread(1)

    chain(1, image)

    @pl.when(chip == 0)
    def _():
        spread(1)

    arrive(1)
    heights = stile[1]
    for t in range(rows - 1):
        heights += gath[1, t]
    proj_one = heights[:, :1]
    weight = jnp.where(lane == 1, proj_one, 0.0)
    keep = jnp.where(jnp.logical_or(lane == 1, lane == 2), 1.0, 0.0)

    def term(x, size):
        y = (x - weight * along(size)) * keep
        return y * y

    squares = term(stile[1], own_square)
    for t in range(rows - 1):
        squares += term(gath[1, t], gath[0, t])
    norm_one = jnp.sqrt(total(squares) + epsilon)
    second = (image - proj_one * first) / norm_one
    pre_two = (pcur[1] - proj_one * pre_one) / norm_one
    image = apply_matrix(1, pre_two)

    stile[2] = jnp.where(
        lane == 0, total(first * image), jnp.where(lane == 1, total(second * image), 0.0)
    )
    spread(2)
    arrive(2)
    heights = stile[2]
    for t in range(rows - 1):
        heights += gath[2, t]
    cross = heights[:, :1]
    proj_two = heights[:, 1:2]
    image = image - cross * first - proj_two * second
    stile[3] = jnp.broadcast_to(total(image * image), (SYS, 128))
    spread(3)
    arrive(3)
    squares = stile[3]
    for t in range(rows - 1):
        squares += gath[3, t]
    norm_two = jnp.sqrt(squares[:, :1] + epsilon)
    weight_one, weight_two = least_squares(beta, proj_one, norm_one, cross, proj_two, norm_two)
    answer = pre_one * weight_one + pre_two * weight_two
    fsend[...] = answer

    def f_copy(t):
        return pltpu.make_async_remote_copy(
            src_ref=fsend, dst_ref=fin.at[t - 1], send_sem=f_send, recv_sem=f_recv,
            device_id=(row, lax.rem(col + t, cols)), device_id_type=MESH,
        )

    @pl.loop(1, cols)
    def _(t):
        f_copy(t).start()

    out[pl.ds(pl.multiple_of(col * SYS, SYS), SYS), :] = answer

    @pl.when(core == 0)
    def _():
        @pl.loop(0, c // tile)
        def _(t):
            to_sibling(t).wait_send()

    for app in range(2):
        @pl.when(core == 0)
        def _():
            c_copy(app).wait_send()

        @pl.when(jnp.logical_and(core == 1, chip < last))
        def _():
            p_copy(app, 0).wait_send()
            p_copy(app, 1).wait_send()

        @pl.when(home != col)
        def _():
            z_copy(app, 0).wait_send()

        @pl.loop(1, rows)
        def _(t):
            z_copy(app, t).wait_send()

        pltpu.make_async_copy(part.at[app], part.at[app], r_send.at[app]).wait()

    for turn in range(4):
        pltpu.make_async_copy(gath.at[turn], gath.at[turn], g_send.at[turn]).wait()

    pltpu.make_async_copy(fin, fin, f_recv).wait()
    for t in range(1, cols):
        at = lax.rem(col + cols - t, cols)
        out[pl.ds(pl.multiple_of(at * SYS, SYS), SYS), :] = fin[t - 1]
    pltpu.make_async_copy(fin, fin, f_send).wait()


def body(rows, cols, rhs, flags, near, far, basis, selft, dinv, low):
    c = dinv.shape[-1]
    per = rows // cols
    tile = min(128, c)
    vm = pltpu.VMEM
    dma = pltpu.SemaphoreType.DMA
    vmem = pl.BlockSpec(memory_space=pltpu.VMEM)
    smem = pl.BlockSpec(memory_space=pltpu.SMEM)
    return pl.pallas_call(
        functools.partial(kernel, rows, cols, tile),
        out_shape=jax.ShapeDtypeStruct(rhs.shape, f32),
        in_specs=[vmem, smem, vmem, vmem, vmem, vmem, vmem, vmem],
        out_specs=vmem,
        scratch_shapes=[
            vm((c, 2 * c), bf16),
            vm((2, c, 2 * c), bf16),
            vm((c, 2 * c), bf16),
            vm((2, SYS, c), f32),
            vm((2, SYS, c), f32),
            vm((SYS, c), f32),
            vm((2, SYS, c), f32),
            vm((2, SYS, c), f32),
            vm((2, 2 * SYS, c // 2), bf16),
            vm((2, per, cols, 2 * SYS, c // 2), bf16),
            vm((2, cols, SYS, c + 128), f32),
            vm((2, cols - 1, SYS, c + 128), f32),
            vm((4, SYS, 128), f32),
            vm((4, rows - 1, SYS, 128), f32),
            vm((SYS, c), f32),
            vm((cols - 1, SYS, c), f32),
            dma((c // tile,)), dma((c // tile,)),
            dma((2,)), dma((2,)),
            dma((2, 2)), dma((2,)),
            dma((2, rows)), dma((2, per)),
            dma((2,)), dma((2,)),
            dma((4,)), dma((4,)),
            dma(()), dma(()),
        ],
        compiler_params=pltpu.CompilerParams(
            collective_id=0, has_side_effects=True, vmem_limit_bytes=40 * 2**20
        ),
    )(rhs, flags, near, far, basis, selft.reshape(1, -1), dinv, low)


def solution(mesh):
    placed = (
        P(None, "row"),
        P("row", "col"),
        P("row", "col", None, None),
        P("row", "col", None, None),
        P("row", None, None),
        P("row"),
        P("row", None, None),
        P("row", None, None),
    )
    return jax.shard_map(
        functools.partial(body, mesh.shape["row"], mesh.shape["col"]),
        mesh=mesh, in_specs=placed, out_specs=P(None, "row"), check_vma=False,
    )
```

time: 1360 us -> 180 us (0.13)
  blocking collectives: 437 us -> 0 us
  waiting for transfers between devices: 365 us -> 0 us
  starting transfers between devices: 320 us -> 0 us
  matrix products: 203 us -> 0 us
  Pallas kernels: 0 us -> 171 us
    psum x8 -> x0, blocking collectives: 437 us -> none  [the longest x3 198 us: project(): height = lax.psum(column_total(direction, image), 'row')]
    ppermute x62 -> x0, starting transfers between devices: 320 us -> none  [from_behind(): return lax.ppermute(block, axis, route)]
    dot_general x132 -> x0, matrix products: 203 us -> none  [the longest x62 125 us: advance(): jnp.dot(previous, lower, precision=highest)]
    pallas_call x0 -> x1, Pallas kernels: none -> 171 us  [body(): pl.pallas_call(functools.partial(kernel, rows, cols, tile), out_shape=jax...]
    all_gather x2 -> x0, waiting for transfers between devices: 152 us -> none  [apply_matrix(): lax.all_gather(solved.astype(jnp.bfloat16), 'row', axis=1, tiled=True)]
    ppermute x62 -> x0, waiting for transfers between devices: 131 us -> none  [from_behind(): return lax.ppermute(block, axis, route)]
    psum x2 -> x0, waiting for transfers between devices: 81.9 us -> none  [apply_matrix(): near_part, far_coef = lax.psum((near_part, far_coef), 'col')]
  transfers between devices with their start and end apart: 66 -> 0, of which waited for: 66 -> 0; matrix products, arithmetic and copies ran while one was open for 0% -> 0% of each run, Pallas kernels for 0% -> 0%
where the time goes in v1:
time: 180 us
  Pallas kernels  171 us (95%)
  local copies, waits for them, and re-layouts  8.72 us (5%)
    pallas_call x1, Pallas kernels, body(): pl.pallas_call(functools.partial(kernel, rows, cols, tile), out_shape=jax...  171 us
    unnamed x17, local copies, waits for them, and re-layouts  8.72 us

profile of v1, /device:TPU:1, one launch (start us, length us, event | category | flops | bytes accessed | tf_op | source)
XLA Modules:
  0.0 179.9 jit_solution(3733493085894602832)
XLA Ops:
  0.0 0.0 copy-start
  0.0 1.6 copy-done
  1.6 0.0 copy-start.1
  1.6 1.2 copy-done.1
  2.8 0.0 copy-start.2
  2.8 1.2 copy-done.2
  4.0 0.0 copy-start.3
  4.0 0.9 copy-done.3
  5.0 0.0 copy-start.4
  5.0 0.9 copy-done.4
  5.9 0.0 copy-start.5
  5.9 0.8 copy-done.5
  6.7 0.0 copy-start.6
  6.7 0.7 copy-done.6
  7.4 0.0 copy-start.7
  7.4 0.7 copy-done.7
  8.1 171.2 %shard_map.82 = f32[64,512]{1,0:T(8,128)S(1)} custom-call(f32[64,512]{1,0:T(8,128)S(1)} %copy-done.4, s32[1,4]{1,0:T(1,128)S(1)} %copy-done.7, bf16[1,4,512,512]{3,2,1,0:T(8,128)(2,1)S(1)} %copy-done, bf16[1,4,64,512]{3,2,1,0:T(8,128)(2,1)S(1)} %copy-done.3, bf16[1,64,512]{2,1,0:T(8,128)(2,1)S(1)} %copy-done.5, f32[1,512]{1,0:T(1,128)S(1)} %bitcast.1, ...), custom_call_target="tpu_custom_call" | custom-call | tf_op jit(solution)/shard_map/pallas_call | solution.py:398
  179.2 0.7 copy.10
Async XLA Ops:
  0.0 1.6 copy-start
  1.6 1.2 copy-start.1
  2.8 1.2 copy-start.2
  4.0 0.9 copy-start.3
  5.0 0.9 copy-start.4
  5.9 0.8 copy-start.5
  6.7 0.7 copy-start.6
  7.4 0.7 copy-start.7

commit v2 on v1

--- a/solution.py
+++ b/solution.py
@@ -12,6 +12,8 @@
 bf16 = jnp.bfloat16
 MESH = pl.DeviceIdType.MESH
 SYS = 8
+GROUP = 4
+HOPS = (2, 0)
 
 
 def stacked(x):
@@ -51,7 +53,9 @@
 
 def kernel(
     rows, cols, tile,
-    rhs, flags, near, far, basis, selft, dinv, low, out,
+    rhs_hbm, flags, near_hbm, far_hbm, basis_hbm, selft_hbm, dinv_hbm, low_hbm, out,
+    rhs, near, far, basis, selft, dinv, low, load,
+    rbuf, sbuf, sol, roots, s_r_send, s_r_recv, s_e_send, s_e_recv, s_p_send,
     dsp, mats, m0, crecv, csend, ebuf, prev, pcur, piece, zbuf, pbuf, part, stile, gath, fsend, fin,
     m_send, m_recv, c_send, c_recv, p_send, p_recv, z_send, z_recv, r_send, r_recv, g_send, g_recv,
     f_send, f_recv,
@@ -65,7 +69,24 @@
     home = row // per
     c = dinv.shape[-1]
     half = c // 2
-    rank = basis.shape[1]
+    rank = basis.shape[0]
+    group = chip // GROUP
+    member = chip % GROUP
+    groups = rows // 2 // GROUP
+    at_end = jnp.logical_and(core == 1, member == GROUP - 1)
+    gives = jnp.logical_and(core == 1, member < GROUP - 1)
+    solver = 2 * GROUP * group + 2 * GROUP - 1
+
+    loads = [
+        pltpu.make_async_copy(source, target, load.at[n])
+        for n, (source, target) in enumerate((
+            (dinv_hbm.at[0], dinv), (low_hbm.at[0], low),
+            (rhs_hbm.at[pl.ds(pl.multiple_of(col * SYS, SYS), SYS)], rhs),
+            (near_hbm.at[0], near), (far_hbm.at[0], far), (basis_hbm.at[0], basis), (selft_hbm, selft),
+        ))
+    ]
+    for copy in loads:
+        copy.start()
 
     bar = pltpu.get_barrier_semaphore()
 
@@ -97,10 +118,24 @@
     def _():
         tell(row - 1, col)
 
+    @pl.when(jnp.logical_not(at_end))
+    def _():
+        tell(solver, col)
+
+    @pl.when(at_end)
+    def _():
+        for y in range(GROUP - 1):
+            tell(2 * GROUP * group + 2 * y + 1, col)
+
+    @pl.when(jnp.logical_and(at_end, group > 0))
+    def _():
+        tell(solver - 2 * GROUP, col)
+
     expected = (rows - 1) + (cols - 1) + rows
     expected = expected - jnp.where(home == col, 1, 0)
     expected = expected + jnp.where(core == 0, 1, jnp.where(chip < last, 2, 0))
-    pl.semaphore_wait(bar, expected)
+    expected = expected + jnp.where(at_end, 2 * GROUP - 1 + jnp.where(group < groups - 1, 1, 0), 0)
+    expected = expected + jnp.where(gives, 1, 0)
 
     def spread(turn):
         @pl.loop(1, rows)
@@ -114,16 +149,25 @@
     def arrive(turn):
         pltpu.make_async_copy(gath.at[turn], gath.at[turn], g_recv.at[turn]).wait()
 
-    v = rhs[pl.ds(pl.multiple_of(col * SYS, SYS), SYS), :]
-    stile[0] = jnp.broadcast_to(total(v * v), (SYS, 128))
-    spread(0)
+    loads[0].wait()
 
     @pl.loop(0, c // tile)
     def _(t):
         at = pl.ds(pl.multiple_of(t * tile, tile), tile)
-        put_split(dsp, at, dinv[0, at, :])
+        put_split(dsp, at, dinv[at, :])
 
     place = 1 - core
+    loads[1].wait()
+
+    @pl.loop(0, c // tile)
+    def _(t):
+        at = pl.ds(pl.multiple_of(t * tile, tile), tile)
+        put_split(mats.at[place], at, times(low[at, :], dsp[...]))
+
+    loads[2].wait()
+    v = rhs[...]
+    stile[0] = jnp.broadcast_to(total(v * v), (SYS, 128))
+    pl.semaphore_wait(bar, expected)
 
     def to_sibling(t):
         at = pl.ds(pl.multiple_of(t * tile, tile), tile)
@@ -133,14 +177,13 @@
             device_id=(row - core + 1, col), device_id_type=MESH,
         )
 
-    @pl.loop(0, c // tile)
-    def _(t):
-        at = pl.ds(pl.multiple_of(t * tile, tile), tile)
-        put_split(mats.at[place], at, times(low[0, at, :], dsp[...]))
-
-        @pl.when(core == 0)
-        def _():
+    @pl.when(core == 0)
+    def _():
+        @pl.loop(0, c // tile)
+        def _(t):
             to_sibling(t).start()
+
+    spread(0)
 
     @pl.when(core == 1)
     def _():
@@ -153,6 +196,16 @@
             y = y[:tile] + y[tile:]
             put_split(mats.at[1], at, y[:, :c] + y[:, c:])
 
+    def matrix_copy(y):
+        return pltpu.make_async_remote_copy(
+            src_ref=mats.at[1], dst_ref=rbuf.at[y], send_sem=s_r_send, recv_sem=s_r_recv.at[y],
+            device_id=(solver, col), device_id_type=MESH,
+        )
+
+    @pl.when(jnp.logical_and(gives, group >= HOPS[0]))
+    def _():
+        matrix_copy(member).start()
+
     sign = jnp.where(core == 0, -1.0, 1.0).astype(f32)
 
     def c_copy(app):
@@ -163,45 +216,136 @@
         )
 
     def p_copy(app, to):
+        target = 2 * chip + 2 + to if to < 2 else solver + 2 * GROUP
         return pltpu.make_async_remote_copy(
             src_ref=pcur.at[app], dst_ref=prev.at[app],
             send_sem=p_send.at[app, to], recv_sem=p_recv.at[app],
-            device_id=(2 * chip + 2 + to, col), device_id_type=MESH,
-        )
+            device_id=(target, col), device_id_type=MESH,
+        )
+
+    def term_copy(app, y):
+        return pltpu.make_async_remote_copy(
+            src_ref=ebuf.at[app], dst_ref=sbuf.at[app, y], send_sem=s_e_send.at[app],
+            recv_sem=s_e_recv.at[app, y], device_id=(solver, col), device_id_type=MESH,
+        )
+
+    def step_copies(app, y):
+        return [
+            pltpu.make_async_remote_copy(
+                src_ref=sol.at[app, y], dst_ref=prev.at[app],
+                send_sem=s_p_send.at[app, 2 * y + k], recv_sem=p_recv.at[app],
+                device_id=(2 * GROUP * group + 2 * y + 2 + k, col), device_id_type=MESH,
+            )
+            for k in range(2 if y < GROUP - 2 else 1)
+        ]
+
+    def both_of(a, b):
+        return jnp.logical_and(a, b)
+
+    def walked(app):
+        return group < HOPS[app]
+
+    def forwards(app):
+        return both_of(chip < last, both_of(core == 1, jnp.logical_or(walked(app), at_end)))
+
+    def leaps(app):
+        return both_of(forwards(app), both_of(at_end, group + 1 >= HOPS[app]))
 
     def chain(app, vec):
         own = times(vec, dsp[...])
+        solved = jnp.logical_not(walked(app))
 
         @pl.when(core == 0)
         def _():
             csend[app] = own
             c_copy(app).start()
-            ebuf[...] = own
+            ebuf[app] = own
 
         @pl.when(core == 1)
         def _():
             c_copy(app).wait_recv()
-            ebuf[...] = own - times(crecv[app], mats[0])
-
-        @pl.when(chip == 0)
-        def _():
-            pcur[app] = ebuf[...]
-
-        @pl.when(chip > 0)
-        def _():
-            p_copy(app, 0).wait_recv()
-            pcur[app] = ebuf[...] + sign * times(prev[app], mats[1])
-
-        @pl.when(jnp.logical_and(core == 1, chip < last))
+            ebuf[app] = own - times(crecv[app], mats[0])
+
+        @pl.when(both_of(gives, solved))
+        def _():
+            term_copy(app, member).start()
+
+        @pl.when(both_of(at_end, solved))
+        def _():
+            if app == 0:
+                for y in range(GROUP - 1):
+                    matrix_copy(y).wait_recv()
+            else:
+                @pl.when(walked(0))
+                def _():
+                    for y in range(GROUP - 1):
+                        matrix_copy(y).wait_recv()
+
+            for y in range(GROUP - 1):
+                term_copy(app, y).wait_recv()
+
+            @pl.when(group == 0)
+            def _():
+                sol[app, 0] = sbuf[app, 0]
+
+            @pl.when(group > 0)
+            def _():
+                p_copy(app, 0).wait_recv()
+                sol[app, 0] = sbuf[app, 0] + times(prev[app], rbuf[0])
+
+            for y in range(GROUP - 1):
+                @pl.when(group == groups - 1)
+                def _():
+                    for copy in step_copies(app, y):
+                        copy.start()
+
+                if y < GROUP - 2:
+                    sol[app, y + 1] = sbuf[app, y + 1] + times(sol[app, y], rbuf[y + 1])
+                else:
+                    pcur[app] = ebuf[app] + times(sol[app, y], mats[1])
+
+        @pl.when(jnp.logical_not(both_of(at_end, solved)))
+        def _():
+            @pl.when(chip == 0)
+            def _():
+                pcur[app] = ebuf[app]
+
+            @pl.when(chip > 0)
+            def _():
+                p_copy(app, 0).wait_recv()
+                pcur[app] = ebuf[app] + sign * times(prev[app], mats[1])
+
+        @pl.when(leaps(app))
+        def _():
+            p_copy(app, 2).start()
+
+        @pl.when(forwards(app))
         def _():
             p_copy(app, 1).start()
             p_copy(app, 0).start()
 
+        @pl.when(both_of(both_of(at_end, solved), group < groups - 1))
+        def _():
+            for y in range(GROUP - 1):
+                for copy in step_copies(app, y):
+                    copy.start()
+
+        if app == 0:
+            @pl.when(both_of(gives, walked(0)))
+            def _():
+                matrix_copy(member).start()
+
+    def far_row(t):
+        return lax.rem(row + t + rows // 2, rows)
+
+    def goes(t):
+        return jnp.logical_or(home != col, far_row(t) != row)
+
     def z_copy(app, t):
         return pltpu.make_async_remote_copy(
             src_ref=piece.at[app], dst_ref=zbuf.at[app, lax.rem(row, per), col],
             send_sem=z_send.at[app, t], recv_sem=z_recv.at[app, lax.rem(row, per)],
-            device_id=(lax.rem(row + t, rows), home), device_id_type=MESH,
+            device_id=(far_row(t), home), device_id_type=MESH,
         )
 
     def r_copy(app, t):
@@ -212,7 +356,7 @@
             device_id=(row, to), device_id_type=MESH,
         )
 
-    def apply_matrix(app, pre):
+    def apply_matrix(app, pre, meanwhile):
         piece[app] = jnp.concatenate([pre[:, :half], pre[:, half:]], axis=0).astype(bf16)
 
         @pl.when(home == col)
@@ -221,13 +365,13 @@
                 piece.at[app], zbuf.at[app, lax.rem(row, per), col], z_recv.at[app, lax.rem(row, per)]
             ).start()
 
-        @pl.when(home != col)
-        def _():
-            z_copy(app, 0).start()
-
-        @pl.loop(1, rows)
+        @pl.loop(0, rows)
         def _(t):
-            z_copy(app, t).start()
+            @pl.when(goes(t))
+            def _():
+                z_copy(app, t).start()
+
+        meanwhile()
 
         near_sum = jnp.zeros((SYS * cols, c), f32)
         far_sum = jnp.zeros((SYS * cols, rank), f32)
@@ -239,9 +383,9 @@
             )
             near_in = z * flags[0, j].astype(f32)
             far_in = (z - near_in).astype(bf16)
-            near_sum += jnp.dot(near_in.astype(bf16), near[0, j], preferred_element_type=f32)
+            near_sum += jnp.dot(near_in.astype(bf16), near[j], preferred_element_type=f32)
             far_sum += lax.dot_general(
-                far_in, far[0, j], (((1,), (1,)), ((), ())), preferred_element_type=f32
+                far_in, far[j], (((1,), (1,)), ((), ())), preferred_element_type=f32
             )
         pbuf[app, :, :, :c] = near_sum.reshape(cols, SYS, c)
         pbuf[app, :, :, c:] = jnp.concatenate(
@@ -257,7 +401,7 @@
         for t in range(cols - 1):
             both += part[app, t]
         far_part = jnp.dot(
-            both[:, c:c + rank].astype(bf16), basis[0], preferred_element_type=f32
+            both[:, c:c + rank].astype(bf16), basis[...], preferred_element_type=f32
         )
         return selft[...] * pre + both[:, :c] + far_part
 
@@ -273,19 +417,30 @@
     first = v / beta
     chain(0, first)
     pre_one = pcur[0]
-    image = apply_matrix(0, pre_one)
-
-    def along(size):
-        return jnp.sqrt(size) / beta_tile
-
-    root = along(own_square)[:, :1]
-    height = total(first * image)
+
+    def wait_loads():
+        for copy in loads[3:]:
+            copy.wait()
+        roots[rows - 1] = jnp.sqrt(own_square) / beta_tile
+        for t in range(rows - 1):
+            roots[t] = jnp.sqrt(gath[0, t]) / beta_tile
+
+    image = apply_matrix(0, pre_one, wait_loads)
+
+    root = roots[rows - 1][:, :1]
     some = root > 1e-15
-    scaled = jnp.where(some, height / jnp.where(some, root, 1.0), 0.0)
-    slope = jnp.where(some, scaled / jnp.where(some, root, 1.0), 0.0)
-    left = image - slope * first
+    unit_one = jnp.where(some, first / jnp.where(some, root, 1.0), 0.0)
+    along = total(unit_one * image)
+    left = image - along * unit_one
     rest = jnp.sqrt(total(left * left))
-    stile[1] = jnp.where(lane == 0, height, jnp.where(lane == 1, scaled, jnp.where(lane == 2, rest, 0.0)))
+
+    def lanes(*values):
+        tile = jnp.zeros((SYS, 128), f32)
+        for at, value in values:
+            tile = jnp.where(lane == at, value, tile)
+        return tile
+
+    stile[1] = lanes((0, total(first * image)), (1, along), (2, rest))
 
     @pl.when(chip > 0)
     def _():
@@ -305,20 +460,39 @@
     weight = jnp.where(lane == 1, proj_one, 0.0)
     keep = jnp.where(jnp.logical_or(lane == 1, lane == 2), 1.0, 0.0)
 
-    def term(x, size):
-        y = (x - weight * along(size)) * keep
+    def term(tile, size):
+        y = (tile - weight * size) * keep
         return y * y
 
-    squares = term(stile[1], own_square)
+    squares = term(stile[1], roots[rows - 1])
     for t in range(rows - 1):
-        squares += term(gath[1, t], gath[0, t])
+        squares += term(gath[1, t], roots[t])
     norm_one = jnp.sqrt(total(squares) + epsilon)
     second = (image - proj_one * first) / norm_one
     pre_two = (pcur[1] - proj_one * pre_one) / norm_one
-    image = apply_matrix(1, pre_two)
-
-    stile[2] = jnp.where(
-        lane == 0, total(first * image), jnp.where(lane == 1, total(second * image), 0.0)
+    frame = []
+
+    def local_frame():
+        turn = total(unit_one * second)
+        across = second - turn * unit_one
+        again = total(unit_one * across)
+        across = across - again * unit_one
+        turn = turn + again
+        size = jnp.sqrt(total(across * across))
+        some = size > 1e-15
+        unit_two = jnp.where(some, across / jnp.where(some, size, 1.0), 0.0)
+        frame.extend((turn, size, unit_two))
+
+    image = apply_matrix(1, pre_two, local_frame)
+    turn, size, unit_two = frame
+    along_one = total(unit_one * image)
+    left = image - along_one * unit_one
+    along_two = total(unit_two * left)
+    left = left - along_two * unit_two
+    stile[2] = lanes(
+        (0, total(first * image)), (1, total(second * image)),
+        (2, along_one), (4, along_two), (6, jnp.sqrt(total(left * left))),
+        (66, turn), (68, size),
     )
     spread(2)
     arrive(2)
@@ -327,14 +501,19 @@
         heights += gath[2, t]
     cross = heights[:, :1]
     proj_two = heights[:, 1:2]
-    image = image - cross * first - proj_two * second
-    stile[3] = jnp.broadcast_to(total(image * image), (SYS, 128))
-    spread(3)
-    arrive(3)
-    squares = stile[3]
+    weight = jnp.where(lane == 2, cross, 0.0)
+    keep = jnp.where(
+        jnp.logical_or(lane == 2, jnp.logical_or(lane == 4, lane == 6)), 1.0, 0.0
+    )
+
+    def term_two(tile, size):
+        y = (tile - weight * size - proj_two * pltpu.roll(tile, 64, 1)) * keep
+        return y * y
+
+    squares = term_two(stile[2], roots[rows - 1])
     for t in range(rows - 1):
-        squares += gath[3, t]
-    norm_two = jnp.sqrt(squares[:, :1] + epsilon)
+        squares += term_two(gath[2, t], roots[t])
+    norm_two = jnp.sqrt(total(squares) + epsilon)
     weight_one, weight_two = least_squares(beta, proj_one, norm_one, cross, proj_two, norm_two)
     answer = pre_one * weight_one + pre_two * weight_two
     fsend[...] = answer
@@ -357,28 +536,44 @@
         def _(t):
             to_sibling(t).wait_send()
 
+    @pl.when(gives)
+    def _():
+        matrix_copy(member).wait_send()
+
     for app in range(2):
         @pl.when(core == 0)
         def _():
             c_copy(app).wait_send()
 
-        @pl.when(jnp.logical_and(core == 1, chip < last))
+        @pl.when(forwards(app))
         def _():
             p_copy(app, 0).wait_send()
             p_copy(app, 1).wait_send()
 
-        @pl.when(home != col)
-        def _():
-            z_copy(app, 0).wait_send()
-
-        @pl.loop(1, rows)
+        @pl.when(leaps(app))
+        def _():
+            p_copy(app, 2).wait_send()
+
+        @pl.when(both_of(gives, jnp.logical_not(walked(app))))
+        def _():
+            term_copy(app, member).wait_send()
+
+        @pl.when(both_of(at_end, jnp.logical_not(walked(app))))
+        def _():
+            for y in range(GROUP - 1):
+                for copy in step_copies(app, y):
+                    copy.wait_send()
+
+        @pl.loop(0, rows)
         def _(t):
-            z_copy(app, t).wait_send()
+            @pl.when(goes(t))
+            def _():
+                z_copy(app, t).wait_send()
 
         pltpu.make_async_copy(part.at[app], part.at[app], r_send.at[app]).wait()
 
-    for turn in range(4):
-        pltpu.make_async_copy(gath.at[turn], gath.at[turn], g_send.at[turn]).wait()
+    for n in range(3):
+        pltpu.make_async_copy(gath.at[n], gath.at[n], g_send.at[n]).wait()
 
     pltpu.make_async_copy(fin, fin, f_recv).wait()
     for t in range(1, cols):
@@ -395,38 +590,47 @@
     dma = pltpu.SemaphoreType.DMA
     vmem = pl.BlockSpec(memory_space=pltpu.VMEM)
     smem = pl.BlockSpec(memory_space=pltpu.SMEM)
+    hbm = pl.BlockSpec(memory_space=pl.ANY)
+    rank = basis.shape[1]
     return pl.pallas_call(
         functools.partial(kernel, rows, cols, tile),
         out_shape=jax.ShapeDtypeStruct(rhs.shape, f32),
-        in_specs=[vmem, smem, vmem, vmem, vmem, vmem, vmem, vmem],
+        in_specs=[hbm, smem] + [hbm] * 6,
         out_specs=vmem,
         scratch_shapes=[
+            vm((SYS, c), f32), vm((per, c, c), bf16), vm((per, rank, c), bf16), vm((rank, c), bf16),
+            vm((1, c), f32), vm((c, c), f32), vm((c, c), f32), dma((7,)),
+            vm((GROUP - 1, c, 2 * c), bf16),
+            vm((2, GROUP - 1, SYS, c), f32),
+            vm((2, GROUP - 1, SYS, c), f32),
+            vm((rows, SYS, 128), f32),
+            dma(()), dma((GROUP - 1,)), dma((2,)), dma((2, GROUP - 1)), dma((2, 2 * GROUP)),
             vm((c, 2 * c), bf16),
             vm((2, c, 2 * c), bf16),
             vm((c, 2 * c), bf16),
             vm((2, SYS, c), f32),
             vm((2, SYS, c), f32),
-            vm((SYS, c), f32),
+            vm((2, SYS, c), f32),
             vm((2, SYS, c), f32),
             vm((2, SYS, c), f32),
             vm((2, 2 * SYS, c // 2), bf16),
             vm((2, per, cols, 2 * SYS, c // 2), bf16),
             vm((2, cols, SYS, c + 128), f32),
             vm((2, cols - 1, SYS, c + 128), f32),
-            vm((4, SYS, 128), f32),
-            vm((4, rows - 1, SYS, 128), f32),
+            vm((3, SYS, 128), f32),
+            vm((3, rows - 1, SYS, 128), f32),
             vm((SYS, c), f32),
             vm((cols - 1, SYS, c), f32),
             dma((c // tile,)), dma((c // tile,)),
             dma((2,)), dma((2,)),
-            dma((2, 2)), dma((2,)),
+            dma((2, 3)), dma((2,)),
             dma((2, rows)), dma((2, per)),
             dma((2,)), dma((2,)),
-            dma((4,)), dma((4,)),
+            dma((3,)), dma((3,)),
             dma(()), dma(()),
         ],
         compiler_params=pltpu.CompilerParams(
-            collective_id=0, has_side_effects=True, vmem_limit_bytes=40 * 2**20
+            collective_id=0, has_side_effects=True, vmem_limit_bytes=60 * 2**20
         ),
     )(rhs, flags, near, far, basis, selft.reshape(1, -1), dinv, low)
 

time: 180 us -> 147 us (0.82)
  Pallas kernels: 171 us -> 145 us
  local copies, waits for them, and re-layouts: 8.72 us -> 1.57 us
    pallas_call x1, Pallas kernels: 171 us -> 145 us  [body(): pl.pallas_call(functools.partial(kernel, rows, cols, tile), out_shape=jax...]
    unnamed x17 -> x1, local copies, waits for them, and re-layouts: 8.72 us -> 1.57 us
where the time goes in v2:
time: 147 us; the launch traced here: 146 us
  Pallas kernels  145 us (99%)
  local copies, waits for them, and re-layouts  1.57 us (1%)
    pallas_call x1, Pallas kernels, body(): pl.pallas_call(functools.partial(kernel, rows, cols, tile), out_shape=jax...  145 us

profile of v2, /device:TPU:1, one launch (start us, length us, event | category | flops | bytes accessed | tf_op | source)
XLA Modules:
  0.0 146.5 jit_solution(15765964092920822170)
XLA Ops:
  0.0 144.9 %shard_map.82 = f32[64,512]{1,0:T(8,128)} custom-call(f32[64,512]{1,0:T(8,128)} %rhs_hbm.1, s32[1,4]{1,0:T(1,128)} %flags.1, bf16[1,4,512,512]{3,2,1,0:T(8,128)(2,1)} %near_hbm.1, bf16[1,4,64,512]{3,2,1,0:T(8,128)(2,1)} %far_hbm.1, bf16[1,64,512]{2,1,0:T(8,128)(2,1)} %basis_hbm.1, f32[1,512]{1,0:T(1,128)} %bitcast.1, f32[1,512,512]{2,1,0:T(8,128)} %dinv_hbm.1, ...), custom_call_target="tpu_custom_call" | custom-call | tf_op jit(solution)/shard_map/pallas_call | solution.py:595
  144.9 1.6 %copy.10 = f32[64,512]{1,0:T(8,128)} copy(f32[64,512]{1,0:T(8,128)} %shard_map.82) | data formatting | bytes 262144

commit v3 on v2

--- a/solution.py
+++ b/solution.py
@@ -56,8 +56,8 @@
     rhs_hbm, flags, near_hbm, far_hbm, basis_hbm, selft_hbm, dinv_hbm, low_hbm, out,
     rhs, near, far, basis, selft, dinv, low, load,
     rbuf, sbuf, sol, roots, s_r_send, s_r_recv, s_e_send, s_e_recv, s_p_send,
-    dsp, mats, m0, crecv, csend, ebuf, prev, pcur, piece, zbuf, pbuf, part, stile, gath, fsend, fin,
-    m_send, m_recv, c_send, c_recv, p_send, p_recv, z_send, z_recv, r_send, r_recv, g_send, g_recv,
+    dsp, mats, m0, crecv, csend, ebuf, prev, pcur, piece, gbuf, zbuf, pbuf, part, stile, gath, fsend, fin,
+    m_send, m_recv, c_send, c_recv, p_send, p_recv, z_send, z_recv, q_send, q_recv, x_send, x_recv, r_send, r_recv, g_send, g_recv,
     f_send, f_recv,
 ):
     row = lax.axis_index("row")
@@ -101,42 +101,6 @@
     def _(t):
         tell(row, lax.rem(col + t, cols))
 
-    @pl.loop(0, rows)
-    def _(t):
-        r = per * col + t // cols
-        k = t % cols
-
-        @pl.when(jnp.logical_or(r != row, k != col))
-        def _():
-            tell(r, k)
-
-    @pl.when(chip > 0)
-    def _():
-        tell(2 * chip - 1, col)
-
-    @pl.when(core == 1)
-    def _():
-        tell(row - 1, col)
-
-    @pl.when(jnp.logical_not(at_end))
-    def _():
-        tell(solver, col)
-
-    @pl.when(at_end)
-    def _():
-        for y in range(GROUP - 1):
-            tell(2 * GROUP * group + 2 * y + 1, col)
-
-    @pl.when(jnp.logical_and(at_end, group > 0))
-    def _():
-        tell(solver - 2 * GROUP, col)
-
-    expected = (rows - 1) + (cols - 1) + rows
-    expected = expected - jnp.where(home == col, 1, 0)
-    expected = expected + jnp.where(core == 0, 1, jnp.where(chip < last, 2, 0))
-    expected = expected + jnp.where(at_end, 2 * GROUP - 1 + jnp.where(group < groups - 1, 1, 0), 0)
-    expected = expected + jnp.where(gives, 1, 0)
-
     def spread(turn):
         @pl.loop(1, rows)
         def _(t):
@@ -167,7 +131,7 @@
     loads[2].wait()
     v = rhs[...]
     stile[0] = jnp.broadcast_to(total(v * v), (SYS, 128))
-    pl.semaphore_wait(bar, expected)
+    pl.semaphore_wait(bar, rows + cols - 2)
 
     def to_sibling(t):
         at = pl.ds(pl.multiple_of(t * tile, tile), tile)
@@ -335,17 +299,37 @@
             def _():
                 matrix_copy(member).start()
 
+    chips = rows // 2
+    count = per // 2
+    side = lax.rem(row, per) // count
+
     def far_row(t):
-        return lax.rem(row + t + rows // 2, rows)
-
-    def goes(t):
-        return jnp.logical_or(home != col, far_row(t) != row)
-
-    def z_copy(app, t):
-        return pltpu.make_async_remote_copy(
-            src_ref=piece.at[app], dst_ref=zbuf.at[app, lax.rem(row, per), col],
-            send_sem=z_send.at[app, t], recv_sem=z_recv.at[app, lax.rem(row, per)],
-            device_id=(far_row(t), home), device_id_type=MESH,
+        return 2 * lax.rem(chip + t + chips // 2, chips) + side
+
+    def piece_copy(app, t):
+        return pltpu.make_async_remote_copy(
+            src_ref=piece.at[app], dst_ref=gbuf.at[app, home, lax.rem(row, count)],
+            send_sem=z_send.at[app, t], recv_sem=z_recv.at[app, home],
+            device_id=(far_row(t), col), device_id_type=MESH,
+        )
+
+    def own_piece_copy(app):
+        return pltpu.make_async_copy(
+            piece.at[app], gbuf.at[app, home, lax.rem(row, count)], z_recv.at[app, home]
+        )
+
+    def plane_copy(app, k):
+        return pltpu.make_async_remote_copy(
+            src_ref=gbuf.at[app, k], dst_ref=zbuf.at[app, core, col],
+            send_sem=q_send.at[app], recv_sem=q_recv.at[app],
+            device_id=(row, k), device_id_type=MESH,
+        )
+
+    def core_copy(app):
+        return pltpu.make_async_remote_copy(
+            src_ref=zbuf.at[app, core], dst_ref=zbuf.at[app, core],
+            send_sem=x_send.at[app], recv_sem=x_recv.at[app],
+            device_id=(row + 1 - 2 * core, col), device_id_type=MESH,
         )
 
     def r_copy(app, t):
@@ -359,34 +343,54 @@
     def apply_matrix(app, pre, meanwhile):
         piece[app] = jnp.concatenate([pre[:, :half], pre[:, half:]], axis=0).astype(bf16)
 
-        @pl.when(home == col)
-        def _():
-            pltpu.make_async_copy(
-                piece.at[app], zbuf.at[app, lax.rem(row, per), col], z_recv.at[app, lax.rem(row, per)]
-            ).start()
-
-        @pl.loop(0, rows)
+        @pl.loop(0, chips)
         def _(t):
-            @pl.when(goes(t))
-            def _():
-                z_copy(app, t).start()
+            @pl.when(far_row(t) != row)
+            def _():
+                piece_copy(app, t).start()
+
+            @pl.when(far_row(t) == row)
+            def _():
+                own_piece_copy(app).start()
 
         meanwhile()
 
-        near_sum = jnp.zeros((SYS * cols, c), f32)
-        far_sum = jnp.zeros((SYS * cols, rank), f32)
-        for j in range(per):
-            pltpu.make_async_copy(zbuf.at[app, j], zbuf.at[app, j], z_recv.at[app, j]).wait()
-            z = zbuf[app, j].astype(f32)
-            z = jnp.concatenate(
-                [z[:, :SYS].reshape(SYS * cols, half), z[:, SYS:].reshape(SYS * cols, half)], axis=1
-            )
-            near_in = z * flags[0, j].astype(f32)
-            far_in = (z - near_in).astype(bf16)
-            near_sum += jnp.dot(near_in.astype(bf16), near[j], preferred_element_type=f32)
-            far_sum += lax.dot_general(
-                far_in, far[j], (((1,), (1,)), ((), ())), preferred_element_type=f32
-            )
+        @pl.loop(0, cols)
+        def _(k):
+            pltpu.make_async_copy(gbuf.at[app, k], gbuf.at[app, k], z_recv.at[app, k]).wait()
+
+            @pl.when(k != col)
+            def _():
+                plane_copy(app, k).start()
+
+            @pl.when(k == col)
+            def _():
+                pltpu.make_async_copy(gbuf.at[app, k], zbuf.at[app, core, col], q_recv.at[app]).start()
+
+        def products(which):
+            near_sum = jnp.zeros((SYS * cols, c), f32)
+            far_sum = jnp.zeros((SYS * cols, rank), f32)
+            for j in range(count):
+                z = zbuf[app, which, :, j].astype(f32)
+                z = jnp.concatenate(
+                    [z[:, :SYS].reshape(SYS * cols, half), z[:, SYS:].reshape(SYS * cols, half)], axis=1
+                )
+                at = which * count + j
+                near_in = z * flags[0, at].astype(f32)
+                far_in = (z - near_in).astype(bf16)
+                near_sum += jnp.dot(near_in.astype(bf16), near[at], preferred_element_type=f32)
+                far_sum += lax.dot_general(
+                    far_in, far[at], (((1,), (1,)), ((), ())), preferred_element_type=f32
+                )
+            return near_sum, far_sum
+
+        pltpu.make_async_copy(zbuf.at[app, core], zbuf.at[app, core], q_recv.at[app]).wait()
+        core_copy(app).start()
+        near_sum, far_sum = products(core)
+        core_copy(app).wait_recv()
+        near_other, far_other = products(1 - core)
+        near_sum += near_other
+        far_sum += far_other
         pbuf[app, :, :, :c] = near_sum.reshape(cols, SYS, c)
         pbuf[app, :, :, c:] = jnp.concatenate(
             [far_sum, jnp.zeros((SYS * cols, 128 - rank), f32)], axis=1
@@ -564,11 +568,15 @@
                 for copy in step_copies(app, y):
                     copy.wait_send()
 
-        @pl.loop(0, rows)
+        @pl.loop(0, chips)
         def _(t):
-            @pl.when(goes(t))
-            def _():
-                z_copy(app, t).wait_send()
+            @pl.when(far_row(t) != row)
+            def _():
+                piece_copy(app, t).wait_send()
+
+        sent = zbuf.at[app, 0, pl.ds(0, cols - 1)]
+        pltpu.make_async_copy(sent, sent, q_send.at[app]).wait()
+        core_copy(app).wait_send()
 
         pltpu.make_async_copy(part.at[app], part.at[app], r_send.at[app]).wait()
 
@@ -614,7 +622,8 @@
             vm((2, SYS, c), f32),
             vm((2, SYS, c), f32),
             vm((2, 2 * SYS, c // 2), bf16),
-            vm((2, per, cols, 2 * SYS, c // 2), bf16),
+            vm((2, cols, per // 2, 2 * SYS, c // 2), bf16),
+            vm((2, 2, cols, per // 2, 2 * SYS, c // 2), bf16),
             vm((2, cols, SYS, c + 128), f32),
             vm((2, cols - 1, SYS, c + 128), f32),
             vm((3, SYS, 128), f32),
@@ -624,7 +633,9 @@
             dma((c // tile,)), dma((c // tile,)),
             dma((2,)), dma((2,)),
             dma((2, 3)), dma((2,)),
-            dma((2, rows)), dma((2, per)),
+            dma((2, rows // 2)), dma((2, cols)),
+            dma((2,)), dma((2,)),
+            dma((2,)), dma((2,)),
             dma((2,)), dma((2,)),
             dma((3,)), dma((3,)),
             dma(()), dma(()),

time: 147 us -> 110 us (0.75)
  Pallas kernels: 145 us -> 108 us
    pallas_call x1, Pallas kernels: 145 us -> 108 us  [body(): pl.pallas_call(functools.partial(kernel, rows, cols, tile), out_shape=jax...]
where the time goes in v3:
time: 110 us
  Pallas kernels  108 us (98%)
  local copies, waits for them, and re-layouts  1.57 us (1%)
    pallas_call x1, Pallas kernels, body(): pl.pallas_call(functools.partial(kernel, rows, cols, tile), out_shape=jax...  108 us

profile of v3, /device:TPU:1, one launch (start us, length us, event | category | flops | bytes accessed | tf_op | source)
XLA Modules:
  0.0 109.7 jit_solution(3075329497593434235)
XLA Ops:
  0.0 108.1 %shard_map.82 = f32[64,512]{1,0:T(8,128)} custom-call(f32[64,512]{1,0:T(8,128)} %rhs_hbm.1, s32[1,4]{1,0:T(1,128)} %flags.1, bf16[1,4,512,512]{3,2,1,0:T(8,128)(2,1)} %near_hbm.1, bf16[1,4,64,512]{3,2,1,0:T(8,128)(2,1)} %far_hbm.1, bf16[1,64,512]{2,1,0:T(8,128)(2,1)} %basis_hbm.1, f32[1,512]{1,0:T(1,128)} %bitcast.1, f32[1,512,512]{2,1,0:T(8,128)} %dinv_hbm.1, ...), custom_call_target="tpu_custom_call" | custom-call | tf_op jit(solution)/shard_map/pallas_call | solution.py:603
  108.1 1.6 %copy.10 = f32[64,512]{1,0:T(8,128)} copy(f32[64,512]{1,0:T(8,128)} %shard_map.82) | data formatting | bytes 262144

commit v4 on v3

--- a/solution.py
+++ b/solution.py
@@ -8,12 +8,13 @@
 from jax.sharding import PartitionSpec as P
 
 epsilon = 1e-06
+SCALE = 2.0 ** -13
 f32 = jnp.float32
 bf16 = jnp.bfloat16
 MESH = pl.DeviceIdType.MESH
 SYS = 8
 GROUP = 4
-HOPS = (2, 0)
+HOPS = (1, 0)
 
 
 def stacked(x):
@@ -55,7 +56,7 @@
     rows, cols, tile,
     rhs_hbm, flags, near_hbm, far_hbm, basis_hbm, selft_hbm, dinv_hbm, low_hbm, out,
     rhs, near, far, basis, selft, dinv, low, load,
-    rbuf, sbuf, sol, roots, s_r_send, s_r_recv, s_e_send, s_e_recv, s_p_send,
+    rbuf, sbuf, sol, roots, pres, blocks, s_q_send, s_q_recv, b_send, b_recv, s_r_send, s_r_recv, s_e_send, s_e_recv, s_p_send,
     dsp, mats, m0, crecv, csend, ebuf, prev, pcur, piece, gbuf, zbuf, pbuf, part, stile, gath, fsend, fin,
     m_send, m_recv, c_send, c_recv, p_send, p_recv, z_send, z_recv, q_send, q_recv, x_send, x_recv, r_send, r_recv, g_send, g_recv,
     f_send, f_recv,
@@ -141,18 +142,35 @@
             device_id=(row - core + 1, col), device_id_type=MESH,
         )
 
+    tiles = c // tile
+    odd = lax.rem(col, 2)
+
+    def tile_at(u):
+        return lax.rem(u + odd * (tiles // 2), tiles)
+
     @pl.when(core == 0)
     def _():
-        @pl.loop(0, c // tile)
-        def _(t):
-            to_sibling(t).start()
+        @pl.loop(0, tiles)
+        def _(u):
+            to_sibling(tile_at(u)).start()
+
+    def half_rows(which):
+        return pl.ds(pl.multiple_of(which * half, half), half)
+
+    def matrix_copy(y):
+        return pltpu.make_async_remote_copy(
+            src_ref=mats.at[1, half_rows(odd)], dst_ref=rbuf.at[y, half_rows(odd)],
+            send_sem=s_r_send, recv_sem=s_r_recv.at[y],
+            device_id=(solver, col), device_id_type=MESH,
+        )
 
     spread(0)
 
     @pl.when(core == 1)
     def _():
-        @pl.loop(0, c // tile)
-        def _(t):
+        @pl.loop(0, tiles)
+        def _(u):
+            t = tile_at(u)
             to_sibling(t).wait_recv()
             at = pl.ds(pl.multiple_of(t * tile, tile), tile)
             both = jnp.concatenate([m0[at, :c], m0[at, c:]], axis=0)
@@ -160,15 +178,32 @@
             y = y[:tile] + y[tile:]
             put_split(mats.at[1], at, y[:, :c] + y[:, c:])
 
-    def matrix_copy(y):
-        return pltpu.make_async_remote_copy(
-            src_ref=mats.at[1], dst_ref=rbuf.at[y], send_sem=s_r_send, recv_sem=s_r_recv.at[y],
-            device_id=(solver, col), device_id_type=MESH,
-        )
-
-    @pl.when(jnp.logical_and(gives, group >= HOPS[0]))
-    def _():
-        matrix_copy(member).start()
+            @pl.when(jnp.logical_and(u == tiles // 2 - 1, jnp.logical_and(gives, group >= HOPS[0])))
+            def _():
+                matrix_copy(member).start()
+
+    quarter = half // 2
+
+    def quarter_rows(which, d):
+        return pl.ds(pl.multiple_of(which * half + d * quarter, quarter), quarter)
+
+    def pass_copy(y, d):
+        at = quarter_rows(odd, d)
+        return pltpu.make_async_remote_copy(
+            src_ref=rbuf.at[y, at], dst_ref=rbuf.at[y, at], send_sem=s_q_send,
+            recv_sem=s_q_recv.at[d, y],
+            device_id=(row, lax.rem(col + (1 if d == 0 else cols - 1), cols)), device_id_type=MESH,
+        )
+
+    def take_matrices():
+        for y in [0] + list(range(GROUP - 2, 0, -1)):
+            matrix_copy(y).wait_recv()
+            for d in range(2):
+                pass_copy(y, d).start()
+        for y in range(GROUP - 1):
+            for d in range(2):
+                there = rbuf.at[y, quarter_rows(1 - odd, d)]
+                pltpu.make_async_copy(there, there, s_q_recv.at[d, y]).wait()
 
     sign = jnp.where(core == 0, -1.0, 1.0).astype(f32)
 
@@ -237,13 +272,7 @@
         @pl.when(both_of(at_end, solved))
         def _():
             if app == 0:
-                for y in range(GROUP - 1):
-                    matrix_copy(y).wait_recv()
-            else:
-                @pl.when(walked(0))
-                def _():
-                    for y in range(GROUP - 1):
-                        matrix_copy(y).wait_recv()
+                take_matrices()
 
             for y in range(GROUP - 1):
                 term_copy(app, y).wait_recv()
@@ -338,6 +367,13 @@
             src_ref=pbuf.at[app, to], dst_ref=part.at[app, t - 1],
             send_sem=r_send.at[app], recv_sem=r_recv.at[app],
             device_id=(row, to), device_id_type=MESH,
+        )
+
+    def block_copy(app, t):
+        return pltpu.make_async_remote_copy(
+            src_ref=pres.at[app], dst_ref=blocks.at[app, t - 1],
+            send_sem=b_send.at[app], recv_sem=b_recv.at[app],
+            device_id=(row, lax.rem(col + t, cols)), device_id_type=MESH,
         )
 
     def apply_matrix(app, pre, meanwhile):
@@ -400,6 +436,10 @@
         def _(t):
             r_copy(app, t).start()
 
+        @pl.loop(1, cols)
+        def _(t):
+            block_copy(app, t).start()
+
         pltpu.make_async_copy(part.at[app], part.at[app], r_recv.at[app]).wait()
         both = pbuf[app, col]
         for t in range(cols - 1):
@@ -411,6 +451,7 @@
 
     lane = lax.broadcasted_iota(jnp.int32, (SYS, 128), 1)
 
+    chain(0, v * SCALE)
     arrive(0)
     own_square = stile[0]
     squares = own_square
@@ -419,8 +460,8 @@
     beta_tile = jnp.sqrt(squares + epsilon)
     beta = beta_tile[:, :1]
     first = v / beta
-    chain(0, first)
-    pre_one = pcur[0]
+    pre_one = pcur[0] * (1.0 / SCALE / beta)
+    pres[0] = pre_one
 
     def wait_loads():
         for copy in loads[3:]:
@@ -428,6 +469,10 @@
         roots[rows - 1] = jnp.sqrt(own_square) / beta_tile
         for t in range(rows - 1):
             roots[t] = jnp.sqrt(gath[0, t]) / beta_tile
+
+        @pl.when(both_of(at_end, walked(0)))
+        def _():
+            take_matrices()
 
     image = apply_matrix(0, pre_one, wait_loads)
 
@@ -474,6 +519,7 @@
     norm_one = jnp.sqrt(total(squares) + epsilon)
     second = (image - proj_one * first) / norm_one
     pre_two = (pcur[1] - proj_one * pre_one) / norm_one
+    pres[1] = pre_two
     frame = []
 
     def local_frame():
@@ -519,8 +565,7 @@
         squares += term_two(gath[2, t], roots[t])
     norm_two = jnp.sqrt(total(squares) + epsilon)
     weight_one, weight_two = least_squares(beta, proj_one, norm_one, cross, proj_two, norm_two)
-    answer = pre_one * weight_one + pre_two * weight_two
-    fsend[...] = answer
+    fsend[...] = lanes((0, weight_one), (1, weight_two))
 
     def f_copy(t):
         return pltpu.make_async_remote_copy(
@@ -532,7 +577,7 @@
     def _(t):
         f_copy(t).start()
 
-    out[pl.ds(pl.multiple_of(col * SYS, SYS), SYS), :] = answer
+    out[pl.ds(pl.multiple_of(col * SYS, SYS), SYS), :] = pre_one * weight_one + pre_two * weight_two
 
     @pl.when(core == 0)
     def _():
@@ -544,6 +589,11 @@
     def _():
         matrix_copy(member).wait_send()
 
+    @pl.when(at_end)
+    def _():
+        passed = rbuf.at[:, pl.ds(0, half)]
+        pltpu.make_async_copy(passed, passed, s_q_send).wait()
+
     for app in range(2):
         @pl.when(core == 0)
         def _():
@@ -579,6 +629,8 @@
         core_copy(app).wait_send()
 
         pltpu.make_async_copy(part.at[app], part.at[app], r_send.at[app]).wait()
+        pltpu.make_async_copy(blocks.at[app], blocks.at[app], b_send.at[app]).wait()
+        pltpu.make_async_copy(blocks.at[app], blocks.at[app], b_recv.at[app]).wait()
 
     for n in range(3):
         pltpu.make_async_copy(gath.at[n], gath.at[n], g_send.at[n]).wait()
@@ -586,7 +638,9 @@
     pltpu.make_async_copy(fin, fin, f_recv).wait()
     for t in range(1, cols):
         at = lax.rem(col + cols - t, cols)
-        out[pl.ds(pl.multiple_of(at * SYS, SYS), SYS), :] = fin[t - 1]
+        out[pl.ds(pl.multiple_of(at * SYS, SYS), SYS), :] = (
+            blocks[0, t - 1] * fin[t - 1, :, 0:1] + blocks[1, t - 1] * fin[t - 1, :, 1:2]
+        )
     pltpu.make_async_copy(fin, fin, f_send).wait()
 
 
@@ -612,6 +666,9 @@
             vm((2, GROUP - 1, SYS, c), f32),
             vm((2, GROUP - 1, SYS, c), f32),
             vm((rows, SYS, 128), f32),
+            vm((2, SYS, c), f32),
+            vm((2, cols - 1, SYS, c), f32),
+            dma(()), dma((2, GROUP - 1)), dma((2,)), dma((2,)),
             dma(()), dma((GROUP - 1,)), dma((2,)), dma((2, GROUP - 1)), dma((2, 2 * GROUP)),
             vm((c, 2 * c), bf16),
             vm((2, c, 2 * c), bf16),
@@ -628,8 +685,8 @@
             vm((2, cols - 1, SYS, c + 128), f32),
             vm((3, SYS, 128), f32),
             vm((3, rows - 1, SYS, 128), f32),
-            vm((SYS, c), f32),
-            vm((cols - 1, SYS, c), f32),
+            vm((SYS, 128), f32),
+            vm((cols - 1, SYS, 128), f32),
             dma((c // tile,)), dma((c // tile,)),
             dma((2,)), dma((2,)),
             dma((2, 3)), dma((2,)),

time: 110 us -> 114 us (1.036)
  Pallas kernels: 108 us -> 112 us
    pallas_call x1, Pallas kernels: 108 us -> 112 us  [body(): pl.pallas_call(functools.partial(kernel, rows, cols, tile), out_shape=jax...]
where the time goes in v4:
time: 114 us; the launch traced here: 113 us
  Pallas kernels  112 us (98%)
  local copies, waits for them, and re-layouts  1.57 us (1%)
    pallas_call x1, Pallas kernels, body(): pl.pallas_call(functools.partial(kernel, rows, cols, tile), out_shape=jax...  112 us

profile of v4, /device:TPU:1, one launch (start us, length us, event | category | flops | bytes accessed | tf_op | source)
XLA Modules:
  0.0 113.5 jit_solution(7790800649526340662)
XLA Ops:
  0.0 111.9 %shard_map.82 = f32[64,512]{1,0:T(8,128)} custom-call(f32[64,512]{1,0:T(8,128)} %rhs_hbm.1, s32[1,4]{1,0:T(1,128)} %flags.1, bf16[1,4,512,512]{3,2,1,0:T(8,128)(2,1)} %near_hbm.1, bf16[1,4,64,512]{3,2,1,0:T(8,128)(2,1)} %far_hbm.1, bf16[1,64,512]{2,1,0:T(8,128)(2,1)} %basis_hbm.1, f32[1,512]{1,0:T(1,128)} %bitcast.1, f32[1,512,512]{2,1,0:T(8,128)} %dinv_hbm.1, ...), custom_call_target="tpu_custom_call" | custom-call | tf_op jit(solution)/shard_map/pallas_call | solution.py:657
  111.9 1.6 %copy.10 = f32[64,512]{1,0:T(8,128)} copy(f32[64,512]{1,0:T(8,128)} %shard_map.82) | data formatting | bytes 262144

commit v5 on v4

--- a/solution.py
+++ b/solution.py
@@ -14,7 +14,7 @@
 MESH = pl.DeviceIdType.MESH
 SYS = 8
 GROUP = 4
-HOPS = (1, 0)
+HOPS = (2, 0)
 
 
 def stacked(x):
@@ -148,12 +148,18 @@
     def tile_at(u):
         return lax.rem(u + odd * (tiles // 2), tiles)
 
-    @pl.when(core == 0)
-    def _():
+    def offer():
         @pl.loop(0, tiles)
         def _(u):
             to_sibling(tile_at(u)).start()
 
+    direct = group == 0
+    late = chip < GROUP // 2
+
+    @pl.when(jnp.logical_and(core == 0, jnp.logical_not(late)))
+    def _():
+        offer()
+
     def half_rows(which):
         return pl.ds(pl.multiple_of(which * half, half), half)
 
@@ -164,10 +170,7 @@
             device_id=(solver, col), device_id_type=MESH,
         )
 
-    spread(0)
-
-    @pl.when(core == 1)
-    def _():
+    def form_pair():
         @pl.loop(0, tiles)
         def _(u):
             t = tile_at(u)
@@ -178,9 +181,13 @@
             y = y[:tile] + y[tile:]
             put_split(mats.at[1], at, y[:, :c] + y[:, c:])
 
-            @pl.when(jnp.logical_and(u == tiles // 2 - 1, jnp.logical_and(gives, group >= HOPS[0])))
+            @pl.when(jnp.logical_and(u == tiles // 2 - 1, jnp.logical_and(gives, group > 0)))
             def _():
                 matrix_copy(member).start()
+
+    @pl.when(jnp.logical_and(core == 1, jnp.logical_not(late)))
+    def _():
+        form_pair()
 
     quarter = half // 2
 
@@ -247,18 +254,28 @@
     def forwards(app):
         return both_of(chip < last, both_of(core == 1, jnp.logical_or(walked(app), at_end)))
 
+    def forwards_to_one(app):
+        return both_of(forwards(app), chip >= GROUP - 1) if app == 0 else forwards(app)
+
     def leaps(app):
         return both_of(forwards(app), both_of(at_end, group + 1 >= HOPS[app]))
 
-    def chain(app, vec):
+    def chain(app, vec, between):
         own = times(vec, dsp[...])
         solved = jnp.logical_not(walked(app))
 
         @pl.when(core == 0)
         def _():
             csend[app] = own
+
+            if app == 0:
+                @pl.when(both_of(direct, chip > 0))
+                def _():
+                    p_copy(app, 0).wait_recv()
+                    csend[app] = own - times(prev[app], mats[1])
+
             c_copy(app).start()
-            ebuf[app] = own
+            ebuf[app] = csend[app]
 
         @pl.when(core == 1)
         def _():
@@ -268,6 +285,8 @@
         @pl.when(both_of(gives, solved))
         def _():
             term_copy(app, member).start()
+
+        between()
 
         @pl.when(both_of(at_end, solved))
         def _():
@@ -299,11 +318,13 @@
 
         @pl.when(jnp.logical_not(both_of(at_end, solved)))
         def _():
-            @pl.when(chip == 0)
+            ready = direct if app == 0 else chip == 0
+
+            @pl.when(ready)
             def _():
                 pcur[app] = ebuf[app]
 
-            @pl.when(chip > 0)
+            @pl.when(jnp.logical_not(ready))
             def _():
                 p_copy(app, 0).wait_recv()
                 pcur[app] = ebuf[app] + sign * times(prev[app], mats[1])
@@ -312,9 +333,12 @@
         def _():
             p_copy(app, 2).start()
 
+        @pl.when(forwards_to_one(app))
+        def _():
+            p_copy(app, 1).start()
+
         @pl.when(forwards(app))
         def _():
-            p_copy(app, 1).start()
             p_copy(app, 0).start()
 
         @pl.when(both_of(both_of(at_end, solved), group < groups - 1))
@@ -323,11 +347,6 @@
                 for copy in step_copies(app, y):
                     copy.start()
 
-        if app == 0:
-            @pl.when(both_of(gives, walked(0)))
-            def _():
-                matrix_copy(member).start()
-
     chips = rows // 2
     count = per // 2
     side = lax.rem(row, per) // count
@@ -369,12 +388,14 @@
             device_id=(row, to), device_id_type=MESH,
         )
 
-    def block_copy(app, t):
-        return pltpu.make_async_remote_copy(
-            src_ref=pres.at[app], dst_ref=blocks.at[app, t - 1],
-            send_sem=b_send.at[app], recv_sem=b_recv.at[app],
-            device_id=(row, lax.rem(col + t, cols)), device_id_type=MESH,
-        )
+    def send_blocks(app):
+        @pl.loop(1, cols)
+        def _(t):
+            pltpu.make_async_remote_copy(
+                src_ref=pres.at[app], dst_ref=blocks.at[app, t - 1],
+                send_sem=b_send.at[app], recv_sem=b_recv.at[app],
+                device_id=(row, lax.rem(col + t, cols)), device_id_type=MESH,
+            ).start()
 
     def apply_matrix(app, pre, meanwhile):
         piece[app] = jnp.concatenate([pre[:, :half], pre[:, half:]], axis=0).astype(bf16)
@@ -436,10 +457,6 @@
         def _(t):
             r_copy(app, t).start()
 
-        @pl.loop(1, cols)
-        def _(t):
-            block_copy(app, t).start()
-
         pltpu.make_async_copy(part.at[app], part.at[app], r_recv.at[app]).wait()
         both = pbuf[app, col]
         for t in range(cols - 1):
@@ -451,7 +468,30 @@
 
     lane = lax.broadcasted_iota(jnp.int32, (SYS, 128), 1)
 
-    chain(0, v * SCALE)
+    def spread_squares():
+        @pl.when(group > 0)
+        def _():
+            spread(0)
+
+    chain(0, v * SCALE, spread_squares)
+
+    @pl.when(group == 0)
+    def _():
+        spread(0)
+
+
+    @pl.when(both_of(late, core == 0))
+    def _():
+        offer()
+
+    @pl.when(both_of(late, core == 1))
+    def _():
+        form_pair()
+
+    @pl.when(both_of(gives, direct))
+    def _():
+        matrix_copy(member).start()
+
     arrive(0)
     own_square = stile[0]
     squares = own_square
@@ -491,15 +531,20 @@
 
     stile[1] = lanes((0, total(first * image)), (1, along), (2, rest))
 
-    @pl.when(chip > 0)
+    first_solver = both_of(at_end, group == 0)
+
+    def spread_heights():
+        @pl.when(jnp.logical_not(first_solver))
+        def _():
+            spread(1)
+            send_blocks(0)
+
+    chain(1, image, spread_heights)
+
+    @pl.when(first_solver)
     def _():
         spread(1)
-
-    chain(1, image)
-
-    @pl.when(chip == 0)
-    def _():
-        spread(1)
+        send_blocks(0)
 
     arrive(1)
     heights = stile[1]
@@ -545,6 +590,7 @@
         (66, turn), (68, size),
     )
     spread(2)
+    send_blocks(1)
     arrive(2)
     heights = stile[2]
     for t in range(rows - 1):
@@ -602,6 +648,9 @@
         @pl.when(forwards(app))
         def _():
             p_copy(app, 0).wait_send()
+
+        @pl.when(forwards_to_one(app))
+        def _():
             p_copy(app, 1).wait_send()
 
         @pl.when(leaps(app))

time: 114 us -> 108 us (0.947)
  Pallas kernels: 112 us -> 106 us
    pallas_call x1, Pallas kernels: 112 us -> 106 us  [body(): pl.pallas_call(functools.partial(kernel, rows, cols, tile), out_shape=jax...]
where the time goes in v5:
time: 108 us
  Pallas kernels  106 us (98%)
  local copies, waits for them, and re-layouts  1.57 us (1%)
    pallas_call x1, Pallas kernels, body(): pl.pallas_call(functools.partial(kernel, rows, cols, tile), out_shape=jax...  106 us

profile of v5, /device:TPU:1, one launch (start us, length us, event | category | flops | bytes accessed | tf_op | source)
XLA Modules:
  0.0 107.5 jit_solution(14365787819921991573)
XLA Ops:
  0.0 106.0 %shard_map.82 = f32[64,512]{1,0:T(8,128)} custom-call(f32[64,512]{1,0:T(8,128)} %rhs_hbm.1, s32[1,4]{1,0:T(1,128)} %flags.1, bf16[1,4,512,512]{3,2,1,0:T(8,128)(2,1)} %near_hbm.1, bf16[1,4,64,512]{3,2,1,0:T(8,128)(2,1)} %far_hbm.1, bf16[1,64,512]{2,1,0:T(8,128)(2,1)} %basis_hbm.1, f32[1,512]{1,0:T(1,128)} %bitcast.1, f32[1,512,512]{2,1,0:T(8,128)} %dinv_hbm.1, ...), custom_call_target="tpu_custom_call" | custom-call | tf_op jit(solution)/shard_map/pallas_call | solution.py:706
  106.0 1.6 %copy.10 = f32[64,512]{1,0:T(8,128)} copy(f32[64,512]{1,0:T(8,128)} %shard_map.82) | data formatting | bytes 262144

commit v6 on v5

--- a/solution.py
+++ b/solution.py
@@ -373,6 +373,8 @@
             device_id=(row, k), device_id_type=MESH,
         )
 
+    far_first = sorted(range(1, cols), key=lambda t: -min(t, cols - t))
+
     def core_copy(app):
         return pltpu.make_async_remote_copy(
             src_ref=zbuf.at[app, core], dst_ref=zbuf.at[app, core],
@@ -389,8 +391,7 @@
         )
 
     def send_blocks(app):
-        @pl.loop(1, cols)
-        def _(t):
+        for t in far_first:
             pltpu.make_async_remote_copy(
                 src_ref=pres.at[app], dst_ref=blocks.at[app, t - 1],
                 send_sem=b_send.at[app], recv_sem=b_recv.at[app],
@@ -453,8 +454,7 @@
             [far_sum, jnp.zeros((SYS * cols, 128 - rank), f32)], axis=1
         ).reshape(cols, SYS, 128)
 
-        @pl.loop(1, cols)
-        def _(t):
+        for t in far_first:
             r_copy(app, t).start()
 
         pltpu.make_async_copy(part.at[app], part.at[app], r_recv.at[app]).wait()
@@ -619,8 +619,7 @@
             device_id=(row, lax.rem(col + t, cols)), device_id_type=MESH,
         )
 
-    @pl.loop(1, cols)
-    def _(t):
+    for t in far_first:
         f_copy(t).start()
 
     out[pl.ds(pl.multiple_of(col * SYS, SYS), SYS), :] = pre_one * weight_one + pre_two * weight_two

time: 108 us -> 106 us (0.981)
  Pallas kernels: 106 us -> 104 us
    pallas_call x1, Pallas kernels: 106 us -> 104 us  [body(): pl.pallas_call(functools.partial(kernel, rows, cols, tile), out_shape=jax...]
where the time goes in v6:
time: 106 us
  Pallas kernels  104 us (98%)
  local copies, waits for them, and re-layouts  1.57 us (1%)
    pallas_call x1, Pallas kernels, body(): pl.pallas_call(functools.partial(kernel, rows, cols, tile), out_shape=jax...  104 us

profile of v6, /device:TPU:1, one launch (start us, length us, event | category | flops | bytes accessed | tf_op | source)
XLA Modules:
  0.0 105.9 jit_solution(9677587755709125355)
XLA Ops:
  0.0 104.4 %shard_map.82 = f32[64,512]{1,0:T(8,128)} custom-call(f32[64,512]{1,0:T(8,128)} %rhs_hbm.1, s32[1,4]{1,0:T(1,128)} %flags.1, bf16[1,4,512,512]{3,2,1,0:T(8,128)(2,1)} %near_hbm.1, bf16[1,4,64,512]{3,2,1,0:T(8,128)(2,1)} %far_hbm.1, bf16[1,64,512]{2,1,0:T(8,128)(2,1)} %basis_hbm.1, f32[1,512]{1,0:T(1,128)} %bitcast.1, f32[1,512,512]{2,1,0:T(8,128)} %dinv_hbm.1, ...), custom_call_target="tpu_custom_call" | custom-call | tf_op jit(solution)/shard_map/pallas_call | solution.py:705
  104.4 1.6 %copy.10 = f32[64,512]{1,0:T(8,128)} copy(f32[64,512]{1,0:T(8,128)} %shard_map.82) | data formatting | bytes 262144

commit v7 on v6

--- a/solution.py
+++ b/solution.py
@@ -8,6 +8,7 @@
 from jax.sharding import PartitionSpec as P
 
 epsilon = 1e-06
+PIECES = 4
 SCALE = 2.0 ** -13
 f32 = jnp.float32
 bf16 = jnp.bfloat16
@@ -160,13 +161,16 @@
     def _():
         offer()
 
-    def half_rows(which):
-        return pl.ds(pl.multiple_of(which * half, half), half)
-
-    def matrix_copy(y):
-        return pltpu.make_async_remote_copy(
-            src_ref=mats.at[1, half_rows(odd)], dst_ref=rbuf.at[y, half_rows(odd)],
-            send_sem=s_r_send, recv_sem=s_r_recv.at[y],
+    piece_rows = half // PIECES
+
+    def part_rows(which, n):
+        return pl.ds(pl.multiple_of(which * half + n * piece_rows, piece_rows), piece_rows)
+
+    def matrix_copy(y, n):
+        at = part_rows(odd, n)
+        return pltpu.make_async_remote_copy(
+            src_ref=mats.at[1, at], dst_ref=rbuf.at[y, at],
+            send_sem=s_r_send, recv_sem=s_r_recv.at[y, n],
             device_id=(solver, col), device_id_type=MESH,
         )
 
@@ -181,36 +185,33 @@
             y = y[:tile] + y[tile:]
             put_split(mats.at[1], at, y[:, :c] + y[:, c:])
 
-            @pl.when(jnp.logical_and(u == tiles // 2 - 1, jnp.logical_and(gives, group > 0)))
-            def _():
-                matrix_copy(member).start()
+            @pl.when(jnp.logical_and(u < tiles // 2, jnp.logical_and(gives, group > 0)))
+            def _():
+                each = PIECES // (tiles // 2)
+                for n in range(each):
+                    matrix_copy(member, u * each + n).start()
 
     @pl.when(jnp.logical_and(core == 1, jnp.logical_not(late)))
     def _():
         form_pair()
 
-    quarter = half // 2
-
-    def quarter_rows(which, d):
-        return pl.ds(pl.multiple_of(which * half + d * quarter, quarter), quarter)
-
-    def pass_copy(y, d):
-        at = quarter_rows(odd, d)
+    def pass_copy(y, n):
+        at = part_rows(odd, n)
         return pltpu.make_async_remote_copy(
             src_ref=rbuf.at[y, at], dst_ref=rbuf.at[y, at], send_sem=s_q_send,
-            recv_sem=s_q_recv.at[d, y],
-            device_id=(row, lax.rem(col + (1 if d == 0 else cols - 1), cols)), device_id_type=MESH,
+            recv_sem=s_q_recv.at[y, n],
+            device_id=(row, lax.rem(col + (1 if n % 2 == 0 else cols - 1), cols)), device_id_type=MESH,
         )
 
     def take_matrices():
-        for y in [0] + list(range(GROUP - 2, 0, -1)):
-            matrix_copy(y).wait_recv()
-            for d in range(2):
-                pass_copy(y, d).start()
-        for y in range(GROUP - 1):
-            for d in range(2):
-                there = rbuf.at[y, quarter_rows(1 - odd, d)]
-                pltpu.make_async_copy(there, there, s_q_recv.at[d, y]).wait()
+        for n in range(PIECES):
+            for y in [0] + list(range(GROUP - 2, 0, -1)):
+                matrix_copy(y, n).wait_recv()
+                pass_copy(y, n).start()
+        for n in range(PIECES):
+            for y in range(GROUP - 1):
+                there = rbuf.at[y, part_rows(1 - odd, n)]
+                pltpu.make_async_copy(there, there, s_q_recv.at[y, n]).wait()
 
     sign = jnp.where(core == 0, -1.0, 1.0).astype(f32)
 
@@ -490,7 +491,8 @@
 
     @pl.when(both_of(gives, direct))
     def _():
-        matrix_copy(member).start()
+        for n in range(PIECES):
+            matrix_copy(member, n).start()
 
     arrive(0)
     own_square = stile[0]
@@ -632,7 +634,8 @@
 
     @pl.when(gives)
     def _():
-        matrix_copy(member).wait_send()
+        given = rbuf.at[0, pl.ds(0, half)]
+        pltpu.make_async_copy(given, given, s_r_send).wait()
 
     @pl.when(at_end)
     def _():
@@ -716,8 +719,8 @@
             vm((rows, SYS, 128), f32),
             vm((2, SYS, c), f32),
             vm((2, cols - 1, SYS, c), f32),
-            dma(()), dma((2, GROUP - 1)), dma((2,)), dma((2,)),
-            dma(()), dma((GROUP - 1,)), dma((2,)), dma((2, GROUP - 1)), dma((2, 2 * GROUP)),
+            dma(()), dma((GROUP - 1, PIECES)), dma((2,)), dma((2,)),
+            dma(()), dma((GROUP - 1, PIECES)), dma((2,)), dma((2, GROUP - 1)), dma((2, 2 * GROUP)),
             vm((c, 2 * c), bf16),
             vm((2, c, 2 * c), bf16),
             vm((c, 2 * c), bf16),

time: 106 us -> 104 us (0.981)
  Pallas kernels: 104 us -> 102 us
    pallas_call x1, Pallas kernels: 104 us -> 102 us  [body(): pl.pallas_call(functools.partial(kernel, rows, cols, tile), out_shape=jax...]
where the time goes in v7:
time: 104 us
  Pallas kernels  102 us (98%)
  local copies, waits for them, and re-layouts  1.57 us (2%)
    pallas_call x1, Pallas kernels, body(): pl.pallas_call(functools.partial(kernel, rows, cols, tile), out_shape=jax...  102 us

profile of v7, /device:TPU:1, one launch (start us, length us, event | category | flops | bytes accessed | tf_op | source)
XLA Modules:
  0.0 103.6 jit_solution(11184162413075575453)
XLA Ops:
  0.0 102.1 %shard_map.82 = f32[64,512]{1,0:T(8,128)} custom-call(f32[64,512]{1,0:T(8,128)} %rhs_hbm.1, s32[1,4]{1,0:T(1,128)} %flags.1, bf16[1,4,512,512]{3,2,1,0:T(8,128)(2,1)} %near_hbm.1, bf16[1,4,64,512]{3,2,1,0:T(8,128)(2,1)} %far_hbm.1, bf16[1,64,512]{2,1,0:T(8,128)(2,1)} %basis_hbm.1, f32[1,512]{1,0:T(1,128)} %bitcast.1, f32[1,512,512]{2,1,0:T(8,128)} %dinv_hbm.1, ...), custom_call_target="tpu_custom_call" | custom-call | tf_op jit(solution)/shard_map/pallas_call | solution.py:708
  102.1 1.6 %copy.10 = f32[64,512]{1,0:T(8,128)} copy(f32[64,512]{1,0:T(8,128)} %shard_map.82) | data formatting | bytes 262144

commit v8 on v7

--- a/solution.py
+++ b/solution.py
@@ -8,7 +8,7 @@
 from jax.sharding import PartitionSpec as P
 
 epsilon = 1e-06
-PIECES = 4
+PIECES = 8
 SCALE = 2.0 ** -13
 f32 = jnp.float32
 bf16 = jnp.bfloat16
@@ -154,7 +154,6 @@
         def _(u):
             to_sibling(tile_at(u)).start()
 
-    direct = group == 0
     late = chip < GROUP // 2
 
     @pl.when(jnp.logical_and(core == 0, jnp.logical_not(late)))
@@ -256,7 +255,7 @@
         return both_of(chip < last, both_of(core == 1, jnp.logical_or(walked(app), at_end)))
 
     def forwards_to_one(app):
-        return both_of(forwards(app), chip >= GROUP - 1) if app == 0 else forwards(app)
+        return both_of(forwards(app), chip >= GROUP // 2 - 1) if app == 0 else forwards(app)
 
     def leaps(app):
         return both_of(forwards(app), both_of(at_end, group + 1 >= HOPS[app]))
@@ -270,7 +269,7 @@
             csend[app] = own
 
             if app == 0:
-                @pl.when(both_of(direct, chip > 0))
+                @pl.when(both_of(late, chip > 0))
                 def _():
                     p_copy(app, 0).wait_recv()
                     csend[app] = own - times(prev[app], mats[1])
@@ -319,7 +318,7 @@
 
         @pl.when(jnp.logical_not(both_of(at_end, solved)))
         def _():
-            ready = direct if app == 0 else chip == 0
+            ready = late if app == 0 else chip == 0
 
             @pl.when(ready)
             def _():
@@ -489,7 +488,7 @@
     def _():
         form_pair()
 
-    @pl.when(both_of(gives, direct))
+    @pl.when(both_of(gives, group == 0))
     def _():
         for n in range(PIECES):
             matrix_copy(member, n).start()

time: 104 us -> 102 us (0.981)
  Pallas kernels: 102 us -> 100 us
    pallas_call x1, Pallas kernels: 102 us -> 100 us  [body(): pl.pallas_call(functools.partial(kernel, rows, cols, tile), out_shape=jax...]
where the time goes in v8:
time: 102 us
  Pallas kernels  100 us (98%)
  local copies, waits for them, and re-layouts  1.57 us (2%)
    pallas_call x1, Pallas kernels, body(): pl.pallas_call(functools.partial(kernel, rows, cols, tile), out_shape=jax...  100 us

profile of v8, /device:TPU:1, one launch (start us, length us, event | category | flops | bytes accessed | tf_op | source)
XLA Modules:
  0.0 101.9 jit_solution(2125299072648721722)
XLA Ops:
  0.0 100.3 %shard_map.82 = f32[64,512]{1,0:T(8,128)} custom-call(f32[64,512]{1,0:T(8,128)} %rhs_hbm.1, s32[1,4]{1,0:T(1,128)} %flags.1, bf16[1,4,512,512]{3,2,1,0:T(8,128)(2,1)} %near_hbm.1, bf16[1,4,64,512]{3,2,1,0:T(8,128)(2,1)} %far_hbm.1, bf16[1,64,512]{2,1,0:T(8,128)(2,1)} %basis_hbm.1, f32[1,512]{1,0:T(1,128)} %bitcast.1, f32[1,512,512]{2,1,0:T(8,128)} %dinv_hbm.1, ...), custom_call_target="tpu_custom_call" | custom-call | tf_op jit(solution)/shard_map/pallas_call | solution.py:707
  100.3 1.6 %copy.10 = f32[64,512]{1,0:T(8,128)} copy(f32[64,512]{1,0:T(8,128)} %shard_map.82) | data formatting | bytes 262144

commit v9 on v8

--- a/solution.py
+++ b/solution.py
@@ -204,7 +204,7 @@
 
     def take_matrices():
         for n in range(PIECES):
-            for y in [0] + list(range(GROUP - 2, 0, -1)):
+            for y in range(GROUP - 1):
                 matrix_copy(y, n).wait_recv()
                 pass_copy(y, n).start()
         for n in range(PIECES):

time: 102 us -> 102 us (level)
  no operation moved by 1% of the time
where the time goes in v9:
time: 102 us
  Pallas kernels  100 us (98%)
  local copies, waits for them, and re-layouts  1.57 us (2%)
    pallas_call x1, Pallas kernels, body(): pl.pallas_call(functools.partial(kernel, rows, cols, tile), out_shape=jax...  100 us

profile of v9, /device:TPU:1, one launch (start us, length us, event | category | flops | bytes accessed | tf_op | source)
XLA Modules:
  0.0 101.9 jit_solution(12928484696779471504)
XLA Ops:
  0.0 100.3 %shard_map.82 = f32[64,512]{1,0:T(8,128)} custom-call(f32[64,512]{1,0:T(8,128)} %rhs_hbm.1, s32[1,4]{1,0:T(1,128)} %flags.1, bf16[1,4,512,512]{3,2,1,0:T(8,128)(2,1)} %near_hbm.1, bf16[1,4,64,512]{3,2,1,0:T(8,128)(2,1)} %far_hbm.1, bf16[1,64,512]{2,1,0:T(8,128)(2,1)} %basis_hbm.1, f32[1,512]{1,0:T(1,128)} %bitcast.1, f32[1,512,512]{2,1,0:T(8,128)} %dinv_hbm.1, ...), custom_call_target="tpu_custom_call" | custom-call | tf_op jit(solution)/shard_map/pallas_call | solution.py:707
  100.3 1.6 %copy.10 = f32[64,512]{1,0:T(8,128)} copy(f32[64,512]{1,0:T(8,128)} %shard_map.82) | data formatting | bytes 262144
